TPU v7x, 256 devices: a whole 4x4x8 slice. The times are simulated.
256 devices in a mesh: wide: 16 (over z, y_hi), narrow: 16 (over y_lo, x, core).
Axes of the slice: x: 4, y: 4 (y_hi: 2, y_lo: 2; y = y_hi * 2 + y_lo), z: 8, core: 2. Of those that a mesh axis runs over, the one named last changes fastest.
Arguments:
- sources: bfloat16 [16384, 1024], P('narrow'), may hold values from -16 to 16
- targets: bfloat16 [32768, 1024], P(('wide', 'narrow')), may hold values from -16 to 16
Outputs:
- row_best: float32 [16384], P('narrow')
- col_best: float32 [32768], P(('wide', 'narrow'))
All inputs are finite; a program needn't handle non-finite values.
Results may differ from a plain program's by a relative error of at most 0.0003.
Values may be sent and summed in bfloat16 or wider, within the bound.
No kernel may reach another device: no remote copies, remote signals or barrier semaphores. Data moves between devices by JAX's collectives and lax.ppermute only.
A program may use at most 64 MiB of HBM per device.

v0:
```python
import functools
import math

import jax
import jax.numpy as jnp
from jax import lax
from jax.experimental import pallas as pl
from jax.experimental.pallas import tpu as pltpu
from jax.sharding import PartitionSpec as P

XS, YS, ZS, CORES = 4, 4, 8, 2
BOTH = ("wide", "narrow")
GROUP = 8
LANES = 128


def device_index(z, y, x, core):
    y, x, z = y % YS, x % XS, z % ZS
    return (z * 2 + y // 2) * 16 + (y % 2) * 8 + x * 2 + core


def places():
    for z in range(ZS):
        for y in range(YS):
            for x in range(XS):
                for core in range(CORES):
                    yield z, y, x, core


def partner(y, core):
    return y ^ 1 if core == 0 else 3 - y


def move(value, where):
    pairs = [(device_index(*place), device_index(*where(*place))) for place in places()]
    return lax.ppermute(value, BOTH, pairs)


def ahead(z, y, x, core):
    return z, y, x + 1 - 2 * core, core


def behind(z, y, x, core):
    return z, y, x - 1 + 2 * core, core


def across(z, y, x, core):
    return z, partner(y, core), x, core


def to_core(z, y, x, core):
    return z, y, x, 1 - core


def column_groups():
    groups = []
    for z in range(ZS):
        for core in range(CORES):
            for y in (0, 2):
                rows = (y, partner(y, core))
                groups.append([device_index(z, row, x, core) for row in rows for x in range(XS)])
    return groups


def vmem():
    return pl.BlockSpec(memory_space=pltpu.VMEM)


def after(values):
    return lax.optimization_barrier(values)


def held(value):
    return pltpu.with_memory_space_constraint(value, pltpu.VMEM)


def call(kernel, out_shape, *operands, flops=0, exps=0, scratch=(), far=(), limit=24):
    moved = sum(math.prod(o.shape) * o.dtype.itemsize for o in operands)
    return pl.pallas_call(
        kernel,
        out_shape=out_shape,
        in_specs=[pl.BlockSpec(memory_space=pltpu.HBM) if k in far else vmem() for k in range(len(operands))],
        out_specs=jax.tree.map(lambda _: vmem(), out_shape),
        scratch_shapes=list(scratch),
        cost_estimate=pl.CostEstimate(flops=flops, bytes_accessed=moved, transcendentals=exps),
        compiler_params=pltpu.CompilerParams(vmem_limit_bytes=limit * 1024 * 1024),
    )(*operands)


def f32(*shape):
    return jax.ShapeDtypeStruct(shape, jnp.float32)


def eye():
    row = lax.broadcasted_iota(jnp.int32, (LANES, LANES), 0)
    return row == lax.broadcasted_iota(jnp.int32, (LANES, LANES), 1)


def as_row(column):
    return jnp.sum(jnp.where(eye(), column, 0.0), axis=0, keepdims=True)


def as_column(row):
    return jnp.sum(jnp.where(eye(), row, 0.0), axis=1, keepdims=True)


def own_place():
    narrow = lax.axis_index("narrow")
    return narrow // 8, (narrow // 2) % 4, narrow % 2


def owner(place, slot):
    y_lo, x, core = place
    dx, dy = slot
    return ((y_lo + dy) % 2) * 4 + (x + 4 + dx * (1 - 2 * core)) % 4


CALLS = (((0, 0), (0, 1)), ((3, 0), (1, 0)), ((3, 1), (2, 0)), ((1, 1), (2, 1)))
SLOTS = tuple((call, k, slot) for call, slots in enumerate(CALLS) for k, slot in enumerate(slots))


def products(scale, s0, s1, targets, scores, row_part):
    count = targets.shape[0]
    rate = scale / math.log(2.0)
    running = None
    for i in range(8):
        source = (s0 if i < 4 else s1)[pl.ds((i % 4) * 256, 256), :]
        part = lax.dot_general(
            targets, source, (((1,), (1,)), ((), ())), preferred_element_type=jnp.float32
        )
        scores[:, pl.ds(i * 256, 256)] = part
        top = jnp.max(part, axis=0, keepdims=True)
        total = jnp.sum(jnp.exp2((part - top) * rate), axis=0, keepdims=True)
        result = top * scale + jnp.log(total)
        row_part[pl.ds(2 * i, 1), :] = result[:, :LANES]
        row_part[pl.ds(2 * i + 1, 1), :] = result[:, LANES:]
        top = jnp.maximum(part[:, :LANES], part[:, LANES:])
        running = top if running is None else jnp.maximum(running, top)
    top = jnp.max(running, axis=1, keepdims=True)
    total = jnp.zeros((count, LANES), jnp.float32)
    for j in range(16):
        total += jnp.exp2((scores[:, pl.ds(j * LANES, LANES)] - top) * rate)
    result = top * scale + jnp.log(jnp.sum(total, axis=1, keepdims=True))
    return [as_row(result[k : k + LANES]) for k in range(0, count, LANES)]


def bring_kernel(sources, targets, sources_here, targets_here, sems):
    copies = [pltpu.make_async_copy(targets, targets_here, sems.at[0])]
    for i in range(8):
        rows = pl.ds(i * 128, 128)
        copies.append(pltpu.make_async_copy(sources.at[rows], sources_here.at[rows], sems.at[i + 1]))
    for copy in copies:
        copy.start()
    for copy in copies:
        copy.wait()


def some_kernel(scale, s0, s1, *refs):
    blocks, (scores, row_part, col_part) = refs[:-3], refs[-3:]
    targets = jnp.concatenate([block[...] for block in blocks], axis=0)
    for k, row in enumerate(products(scale, s0, s1, targets, scores, row_part)):
        col_part[pl.ds(k, 1), :] = row


def end_kernel(scale, s0, s1, ta, tb, *refs):
    rows, cols = refs[:3], refs[3:6]
    scores, joint, sent, scratch, last = refs[6:]
    targets = jnp.concatenate([ta[...], tb[...]], axis=0)
    ends = products(scale, s0, s1, targets, scores, last)
    joint[...] = log_sum([row[...] for row in rows] + [last[...]])
    place = own_place()
    for call, k, slot in SLOTS:
        row = ends[k] if call == 3 else cols[call][pl.ds(k, 1), :]
        scratch[pl.ds(owner(place, slot), 1), :] = row
    whole = scratch[...]
    for e in range(GROUP):
        sent[pl.ds(e * GROUP, GROUP), :] = whole


def log_sum(parts):
    top = functools.reduce(jnp.maximum, parts)
    return top + jnp.log(sum(jnp.exp(part - top) for part in parts))


def row_best_kernel(scale, a0, a1, a2, a3, received, row_joint, rows, col_norm):
    norm = log_sum([received[pl.ds(e * GROUP, GROUP), :] for e in range(GROUP)])
    col_norm[...] = norm
    place = own_place()
    half = 0.5 / scale
    best = [None] * 16
    for call, k, slot in SLOTS:
        column = as_column(col_norm[pl.ds(owner(place, slot), 1), :]) * half
        column = jnp.broadcast_to(column, (LANES, LANES))
        block = (a0, a1, a2, a3)[call]
        for j in range(16):
            part = block[pl.ds(k * LANES, LANES), pl.ds(j * LANES, LANES)] - column
            part = functools.reduce(jnp.maximum, [part[8 * q : 8 * q + 8] for q in range(16)])
            best[j] = part if best[j] is None else jnp.maximum(best[j], part)
    rows[:16] = row_joint[...]
    for j in range(16):
        rows[pl.ds(16 + j, 1), :] = jnp.max(best[j], axis=0, keepdims=True) * scale


def join_kernel(rows, incoming, sent):
    norm_own = log_sum([rows[:8], incoming[8:16]])
    norm_other = log_sum([rows[8:16], incoming[:8]])
    best_own = jnp.maximum(rows[16:24], incoming[24:])
    best_other = jnp.maximum(rows[24:], incoming[16:24])
    for e in range(16):
        for k, value in enumerate((norm_own, norm_other, best_own, best_other)):
            sent[pl.ds(e * 32 + k * 8, 8), :] = value


def col_best_kernel(scale, a0, a1, a2, a3, received, col_norm, sent, row_best):
    parts = [received[pl.ds(e * 32, 16), :] for e in range(16)]
    row_norm = log_sum(parts)
    best = functools.reduce(jnp.maximum, [received[pl.ds(e * 32 + 16, 8), :] for e in range(16)])
    row_best[...] = best - 0.5 * row_norm[:8]
    place = own_place()
    norms = row_norm * (0.5 / scale)
    for call, k, slot in SLOTS:
        block = (a0, a1, a2, a3)[call]
        best = None
        for j in range(16):
            part = block[pl.ds(k * LANES, LANES), pl.ds(j * LANES, LANES)] - norms[j : j + 1, :]
            best = part if best is None else jnp.maximum(best, part)
        best = as_row(jnp.max(best, axis=1, keepdims=True)) * scale
        position = owner(place, slot)
        sent[pl.ds(position, 1), :] = best - 0.5 * col_norm[pl.ds(position, 1), :]


def last_kernel(received, row_best_held, row_best, col_best):
    row_best[...] = row_best_held[...]
    col_best[...] = jnp.max(received[...], axis=0, keepdims=True)


def body(sources, targets):
    scale = 1.0 / math.sqrt(sources.shape[1])
    groups = column_groups()

    def exchange(value):
        return lax.all_to_all(value, BOTH, 0, 0, axis_index_groups=groups, tiled=True)

    def kept(rows):
        return pltpu.VMEM((rows, 2048), jnp.float32)

    blocks = {}
    blocks[3, 0] = move(targets, ahead)
    blocks[0, 1] = move(targets, across)
    other = held(move(sources, to_core))
    sources, blocks[0, 0] = call(
        bring_kernel,
        (pltpu.VMEM((1024, 1024), jnp.bfloat16), pltpu.VMEM((LANES, 1024), jnp.bfloat16)),
        pltpu.with_memory_space_constraint(sources, pltpu.HBM),
        pltpu.with_memory_space_constraint(targets, pltpu.HBM),
        far=(0, 1),
        scratch=[pltpu.SemaphoreType.DMA((9,))],
    )
    blocks[1, 0] = move(blocks[0, 0], behind)
    blocks[3, 0], blocks[0, 0] = after((blocks[3, 0], blocks[0, 0]))
    blocks[2, 0] = move(blocks[3, 0], ahead)
    blocks[3, 1] = move(blocks[3, 0], across)
    both = (held(sources), other)

    scores, rows, cols = [], [], []
    for n, slots in enumerate(CALLS[:-1]):
        count = len(slots) * LANES
        if n == 1:
            blocks[1, 0], rows[0] = after((blocks[1, 0], rows[0]))
            blocks[1, 1] = move(blocks[1, 0], across)
        if n == 2:
            blocks[2, 0], rows[1] = after((blocks[2, 0], rows[1]))
            blocks[2, 1] = move(blocks[2, 0], across)
        part, row, col = call(
            functools.partial(some_kernel, scale),
            (kept(count), f32(16, LANES), f32(len(slots), LANES)),
            *both,
            *[blocks[slot] for slot in slots],
            flops=2 * count * 2048 * 1024,
            exps=2 * count * 2048,
        )
        scores.append(held(part))
        rows.append(row)
        cols.append(col)
    part, row_joint, sent = call(
        functools.partial(end_kernel, scale),
        (kept(2 * LANES), f32(16, LANES), f32(GROUP * GROUP, LANES)),
        *both,
        *[blocks[slot] for slot in CALLS[-1]],
        *rows,
        *cols,
        flops=4 * LANES * 2048 * 1024,
        exps=4 * LANES * 2048,
        scratch=[pltpu.VMEM((GROUP, LANES), jnp.float32), pltpu.VMEM((16, LANES), jnp.float32)],
    )
    scores.append(held(part))
    received = exchange(sent)
    joint, col_norm = call(
        functools.partial(row_best_kernel, scale),
        (f32(32, LANES), f32(GROUP, LANES)),
        *scores,
        received,
        row_joint,
        flops=2 * 1024 * 2048,
    )
    sent = call(join_kernel, f32(512, LANES), joint, move(joint, to_core))
    received = lax.all_to_all(sent, "wide", 0, 0, tiled=True)
    sent, row_best = call(
        functools.partial(col_best_kernel, scale),
        (f32(GROUP, LANES), pltpu.VMEM((8, LANES), jnp.float32)),
        *scores,
        received,
        col_norm,
        flops=2 * 1024 * 2048,
    )
    received = exchange(sent)
    row_best, col_best = call(
        last_kernel, (f32(8, LANES), f32(1, LANES)), received, held(row_best)
    )
    return row_best.reshape(1024), col_best.reshape(LANES)


def solution(mesh):
    return jax.shard_map(
        body,
        mesh=mesh,
        in_specs=(P("narrow", None), P(("wide", "narrow"), None)),
        out_specs=(P("narrow"), P(("wide", "narrow"))),
        check_vma=False,
    )
```

profile of v0, /device:TPU:1, one launch (start us, length us, event | category | flops | bytes accessed | tf_op | source)
XLA Modules:
  0.0 72.2 jit_solution(5015324806876441433)
XLA Ops:
  0.6 3.3 %collective-permute-start = (bf16[1024,1024]{1,0:T(8,128)(2,1)}, bf16[1024,1024]{1,0:T(8,128)(2,1)S(1)}, u32[]{:S(2)}, u32[]{:S(2)}) collective-permute-start(bf16[1024,1024]{1,0:T(8,128)(2,1)} %sources.1), channel_id=1, source_target_pairs={{0,1},{1,0},{2,3},{3,2},{4,5},{5,4},{6,7},{7,6},{8,9},{9,8},{10,11... | collective-permute-start | bytes 6291464 | tf_op jit(solution)/shard_map/ppermute | solution.py:36
  4.0 0.7 %collective-permute-start.1 = (bf16[128,1024]{1,0:T(8,128)(2,1)}, bf16[128,1024]{1,0:T(8,128)(2,1)S(1)}, u32[]{:S(2)}, u32[]{:S(2)}) collective-permute-start(bf16[128,1024]{1,0:T(8,128)(2,1)} %targets.1), channel_id=1, source_target_pairs={{0,2},{1,7},{2,4},{3,1},{4,6},{5,3},{6,0},{7,5},{8,10},{9,15},{10,... | collective-permute-start | bytes 786440 | tf_op jit(solution)/shard_map/ppermute | solution.py:36
  4.7 2.7 %collective-permute-start.2 = (bf16[128,1024]{1,0:T(8,128)(2,1)}, bf16[128,1024]{1,0:T(8,128)(2,1)S(1)}, u32[]{:S(2)}, u32[]{:S(2)}) collective-permute-start(bf16[128,1024]{1,0:T(8,128)(2,1)} %targets.1), channel_id=1, source_target_pairs={{0,8},{1,25},{2,10},{3,27},{4,12},{5,29},{6,14},{7,31},{8,0},{9,17... | collective-permute-start | bytes 786440 | tf_op jit(solution)/shard_map/ppermute | solution.py:36
  7.4 1.7 %shard_map.41 = (bf16[1024,1024]{1,0:T(8,128)(2,1)S(1)}, bf16[128,1024]{1,0:T(8,128)(2,1)S(1)}) custom-call(bf16[1024,1024]{1,0:T(8,128)(2,1)} %sources.1, bf16[128,1024]{1,0:T(8,128)(2,1)} %targets.1), custom_call_target="tpu_custom_call" | custom-call | bytes 2359296 | tf_op jit(solution)/shard_map/pallas_call | solution.py:79
  9.1 0.1 collective-permute-start.3
  9.2 0.5 collective-permute-done.1.refs_0_
  9.7 2.2 %collective-permute-start.5 = (bf16[128,1024]{1,0:T(8,128)(2,1)S(1)}, bf16[128,1024]{1,0:T(8,128)(2,1)S(1)}, u32[]{:S(2)}, u32[]{:S(2)}) collective-permute-start(bf16[128,1024]{1,0:T(8,128)(2,1)S(1)} %collective-permute-done.1.refs_0_), channel_id=1, source_target_pairs={{0,2},{1,7},{2,4},{3,1},{4,6},{5,3},{6,0},{7,5},{8,10},{9,15},{10,... | collective-permute-start | bytes 786440 | tf_op jit(solution)/shard_map/ppermute | solution.py:36
  11.9 2.2 %collective-permute-start.4 = (bf16[128,1024]{1,0:T(8,128)(2,1)S(1)}, bf16[128,1024]{1,0:T(8,128)(2,1)S(1)}, u32[]{:S(2)}, u32[]{:S(2)}) collective-permute-start(bf16[128,1024]{1,0:T(8,128)(2,1)S(1)} %collective-permute-done.1.refs_0_), channel_id=1, source_target_pairs={{0,8},{1,25},{2,10},{3,27},{4,12},{5,29},{6,14},{7,31},{8,0},{9,17... | collective-permute-start | bytes 786440 | tf_op jit(solution)/shard_map/ppermute | solution.py:36
  14.1 0.0 collective-permute-done.2.refs_1_
  14.1 0.0 collective-permute-done.s1
  14.1 2.0 %shard_map.42 = (f32[256,2048]{1,0:T(8,128)S(1)}, f32[16,128]{1,0:T(8,128)S(1)}, f32[2,128]{1,0:T(2,128)S(1)}) custom-call(bf16[1024,1024]{1,0:T(8,128)(2,1)S(1)} %get-tuple-element.28.s0, bf16[1024,1024]{1,0:T(8,128)(2,1)S(1)} %collective-permute-done.s1, bf16[128,1024]{1,0:T(8,128)(2,1)S(1)} %get-tuple-element.30.refs_0_, ...), custom_call_target="tpu_custom_call" | custom-call | flops 1073741824 | bytes 4718592 | tf_op jit(solution)/shard_map/pallas_call | solution.py:79
  16.1 0.0 collective-permute-done.3.refs_1_
  16.1 0.5 collective-permute-start.6
  16.7 2.0 %shard_map.43 = (f32[256,2048]{1,0:T(8,128)S(1)}, f32[16,128]{1,0:T(8,128)S(1)}, f32[2,128]{1,0:T(2,128)S(1)}) custom-call(bf16[1024,1024]{1,0:T(8,128)(2,1)S(1)} %get-tuple-element.28.s0, bf16[1024,1024]{1,0:T(8,128)(2,1)S(1)} %collective-permute-done.s1, bf16[128,1024]{1,0:T(8,128)(2,1)S(1)} %collective-permute-done.1.refs_0_, ...), custom_call_target="tpu_custom_call" | custom-call | flops 1073741824 | bytes 4718592 | tf_op jit(solution)/shard_map/pallas_call | solution.py:79
  18.7 0.0 collective-permute-done.5.refs_1_
  18.7 2.3 %collective-permute-start.7 = (bf16[128,1024]{1,0:T(8,128)(2,1)S(1)}, bf16[128,1024]{1,0:T(8,128)(2,1)S(1)}, u32[]{:S(2)}, u32[]{:S(2)}) collective-permute-start(bf16[128,1024]{1,0:T(8,128)(2,1)S(1)} %collective-permute-done.5.refs_1_), channel_id=1, source_target_pairs={{0,8},{1,25},{2,10},{3,27},{4,12},{5,29},{6,14},{7,31},{8,0},{9,17... | collective-permute-start | bytes 786440 | tf_op jit(solution)/shard_map/ppermute | solution.py:36
  21.0 0.0 collective-permute-done.4.refs_0_
  21.0 2.0 %shard_map.44 = (f32[256,2048]{1,0:T(8,128)S(1)}, f32[16,128]{1,0:T(8,128)S(1)}, f32[2,128]{1,0:T(2,128)S(1)}) custom-call(bf16[1024,1024]{1,0:T(8,128)(2,1)S(1)} %get-tuple-element.28.s0, bf16[1024,1024]{1,0:T(8,128)(2,1)S(1)} %collective-permute-done.s1, bf16[128,1024]{1,0:T(8,128)(2,1)S(1)} %collective-permute-done.4.refs_0_, ...), custom_call_target="tpu_custom_call" | custom-call | flops 1073741824 | bytes 4718592 | tf_op jit(solution)/shard_map/pallas_call | solution.py:79
  23.1 0.0 collective-permute-done.6.ta
  23.1 2.4 %collective-permute-done.7.tb = bf16[128,1024]{1,0:T(8,128)(2,1)S(1)} collective-permute-done((bf16[128,1024]{1,0:T(8,128)(2,1)S(1)}, bf16[128,1024]{1,0:T(8,128)(2,1)S(1)}, u32[]{:S(2)}, u32[]{:S(2)}) %collective-permute-start.7) | collective-permute-done | bytes 262176 | tf_op jit(solution)/shard_map/ppermute | solution.py:36
  25.5 2.0 %shard_map.45 = (f32[256,2048]{1,0:T(8,128)S(1)}, f32[16,128]{1,0:T(8,128)S(1)}, f32[64,128]{1,0:T(8,128)S(1)}) custom-call(bf16[1024,1024]{1,0:T(8,128)(2,1)S(1)} %get-tuple-element.28.s0, bf16[1024,1024]{1,0:T(8,128)(2,1)S(1)} %collective-permute-done.s1, bf16[128,1024]{1,0:T(8,128)(2,1)S(1)} %collective-permute-done.6.ta, ...), custom_call_target="tpu_custom_call" | custom-call | flops 1073741824 | bytes 4746240 | tf_op jit(solution)/shard_map/pallas_call | solution.py:79
  27.5 9.6 %all_to_all.33 = f32[8,8,128]{2,1,0:T(8,128)S(1)} all-to-all(f32[8,8,128]{2,1,0:T(8,128)S(1)} %bitcast.13), channel_id=1, replica_groups={{0,2,4,6,8,10,12,14},{16,18,20,22,24,26,28,30},{1,3,5,7,25,27,29,31},{1..., dimensions={0} | all-to-all | bytes 65536 | tf_op jit(solution)/shard_map/all_to_all | solution.py:242
  37.1 0.8 %shard_map.46 = (f32[32,128]{1,0:T(8,128)S(1)}, f32[8,128]{1,0:T(8,128)S(1)}) custom-call(f32[256,2048]{1,0:T(8,128)S(1)} %get-tuple-element.31.a0, f32[256,2048]{1,0:T(8,128)S(1)} %get-tuple-element.35.a1, f32[256,2048]{1,0:T(8,128)S(1)} %get-tuple-element.38.a2, f32[256,2048]{1,0:T(8,128)S(1)} %get-tuple-element.45.a3, f32[64,128]{1,0:T(8,128)S(1)} %bitcast.12, ...), custom_call_target="tpu_custom_call" | custom-call | flops 4194304 | bytes 8429568 | tf_op jit(solution)/shard_map/pallas_call | solution.py:79
  37.8 0.9 %collective-permute-start.8 = (f32[32,128]{1,0:T(8,128)S(1)}, f32[32,128]{1,0:T(8,128)S(1)}, u32[]{:S(2)}, u32[]{:S(2)}) collective-permute-start(f32[32,128]{1,0:T(8,128)S(1)} %get-tuple-element.48.rows), channel_id=1, source_target_pairs={{0,1},{1,0},{2,3},{3,2},{4,5},{5,4},{6,7},{7,6},{8,9},{9,8},{10,11... | collective-permute-start | bytes 49160 | tf_op jit(solution)/shard_map/ppermute | solution.py:36
  38.7 0.8 %collective-permute-done.8.incoming = f32[32,128]{1,0:T(8,128)S(1)} collective-permute-done((f32[32,128]{1,0:T(8,128)S(1)}, f32[32,128]{1,0:T(8,128)S(1)}, u32[]{:S(2)}, u32[]{:S(2)}) %collective-permute-start.8) | collective-permute-done | bytes 16416 | tf_op jit(solution)/shard_map/ppermute | solution.py:36
  39.6 22.7 %all_to_all.34 = f32[16,32,128]{2,1,0:T(8,128)S(1)} all-to-all(f32[16,32,128]{2,1,0:T(8,128)S(1)} %bitcast.11), channel_id=1, replica_groups=mesh['wide'=16,'narrow'=16] {'wide'}, dimensions={0} | all-to-all | bytes 524288 | tf_op jit(solution)/shard_map/all_to_all | solution.py:307
  62.2 0.7 %shard_map.48 = (f32[8,128]{1,0:T(8,128)S(1)}, f32[8,128]{1,0:T(8,128)S(1)}) custom-call(f32[256,2048]{1,0:T(8,128)S(1)} %get-tuple-element.31.a0, f32[256,2048]{1,0:T(8,128)S(1)} %get-tuple-element.35.a1, f32[256,2048]{1,0:T(8,128)S(1)} %get-tuple-element.38.a2, f32[256,2048]{1,0:T(8,128)S(1)} %get-tuple-element.45.a3, f32[512,128]{1,0:T(8,128)S(1)} %bitcast.10, ...), custom_call_target="tpu_custom_call" | custom-call | flops 4194304 | bytes 8654848 | tf_op jit(solution)/shard_map/pallas_call | solution.py:79
  63.0 8.6 %all_to_all.35 = f32[8,1,128]{2,1,0:T(1,128)S(1)} all-to-all(f32[8,1,128]{2,1,0:T(1,128)S(1)} %bitcast.15), channel_id=1, replica_groups={{0,2,4,6,8,10,12,14},{16,18,20,22,24,26,28,30},{1,3,5,7,25,27,29,31},{1..., dimensions={0} | all-to-all | bytes 8192 | tf_op jit(solution)/shard_map/all_to_all | solution.py:242
  71.6 0.6 shard_map.49
  (1 shorter events, 0.0 us)
Async XLA Ops:
  0.6 13.5 %collective-permute-start = (bf16[1024,1024]{1,0:T(8,128)(2,1)}, bf16[1024,1024]{1,0:T(8,128)(2,1)S(1)}, u32[]{:S(2)}, u32[]{:S(2)}) collective-permute-start(bf16[1024,1024]{1,0:T(8,128)(2,1)} %sources.1), channel_id=1, source_target_pairs={{0,1},{1,0},{2,3},{3,2},{4,5},{5,4},{6,7},{7,6},{8,9},{9,8},{10,11... | collective-permute-start | bytes 6291464 | tf_op jit(solution)/shard_map/ppermute | solution.py:36
  4.0 5.7 %collective-permute-start.1 = (bf16[128,1024]{1,0:T(8,128)(2,1)}, bf16[128,1024]{1,0:T(8,128)(2,1)S(1)}, u32[]{:S(2)}, u32[]{:S(2)}) collective-permute-start(bf16[128,1024]{1,0:T(8,128)(2,1)} %targets.1), channel_id=1, source_target_pairs={{0,2},{1,7},{2,4},{3,1},{4,6},{5,3},{6,0},{7,5},{8,10},{9,15},{10,... | collective-permute-start | bytes 786440 | tf_op jit(solution)/shard_map/ppermute | solution.py:36
  4.7 9.4 %collective-permute-start.2 = (bf16[128,1024]{1,0:T(8,128)(2,1)}, bf16[128,1024]{1,0:T(8,128)(2,1)S(1)}, u32[]{:S(2)}, u32[]{:S(2)}) collective-permute-start(bf16[128,1024]{1,0:T(8,128)(2,1)} %targets.1), channel_id=1, source_target_pairs={{0,8},{1,25},{2,10},{3,27},{4,12},{5,29},{6,14},{7,31},{8,0},{9,17... | collective-permute-start | bytes 786440 | tf_op jit(solution)/shard_map/ppermute | solution.py:36
  9.1 7.0 %collective-permute-start.3 = (bf16[128,1024]{1,0:T(8,128)(2,1)S(1)}, bf16[128,1024]{1,0:T(8,128)(2,1)S(1)}, u32[]{:S(2)}, u32[]{:S(2)}) collective-permute-start(bf16[128,1024]{1,0:T(8,128)(2,1)S(1)} %get-tuple-element.30.refs_0_), channel_id=1, source_target_pairs={{0,6},{1,3},{2,0},{3,5},{4,2},{5,7},{6,4},{7,1},{8,14},{9,11},{10,... | collective-permute-start | bytes 786440 | tf_op jit(solution)/shard_map/ppermute | solution.py:36
  9.7 9.0 %collective-permute-start.5 = (bf16[128,1024]{1,0:T(8,128)(2,1)S(1)}, bf16[128,1024]{1,0:T(8,128)(2,1)S(1)}, u32[]{:S(2)}, u32[]{:S(2)}) collective-permute-start(bf16[128,1024]{1,0:T(8,128)(2,1)S(1)} %collective-permute-done.1.refs_0_), channel_id=1, source_target_pairs={{0,2},{1,7},{2,4},{3,1},{4,6},{5,3},{6,0},{7,5},{8,10},{9,15},{10,... | collective-permute-start | bytes 786440 | tf_op jit(solution)/shard_map/ppermute | solution.py:36
  11.9 9.2 %collective-permute-start.4 = (bf16[128,1024]{1,0:T(8,128)(2,1)S(1)}, bf16[128,1024]{1,0:T(8,128)(2,1)S(1)}, u32[]{:S(2)}, u32[]{:S(2)}) collective-permute-start(bf16[128,1024]{1,0:T(8,128)(2,1)S(1)} %collective-permute-done.1.refs_0_), channel_id=1, source_target_pairs={{0,8},{1,25},{2,10},{3,27},{4,12},{5,29},{6,14},{7,31},{8,0},{9,17... | collective-permute-start | bytes 786440 | tf_op jit(solution)/shard_map/ppermute | solution.py:36
  16.1 6.9 %collective-permute-start.6 = (bf16[128,1024]{1,0:T(8,128)(2,1)S(1)}, bf16[128,1024]{1,0:T(8,128)(2,1)S(1)}, u32[]{:S(2)}, u32[]{:S(2)}) collective-permute-start(bf16[128,1024]{1,0:T(8,128)(2,1)S(1)} %collective-permute-done.3.refs_1_), channel_id=1, source_target_pairs={{0,8},{1,25},{2,10},{3,27},{4,12},{5,29},{6,14},{7,31},{8,0},{9,17... | collective-permute-start | bytes 786440 | tf_op jit(solution)/shard_map/ppermute | solution.py:36
  18.7 6.7 %collective-permute-start.7 = (bf16[128,1024]{1,0:T(8,128)(2,1)S(1)}, bf16[128,1024]{1,0:T(8,128)(2,1)S(1)}, u32[]{:S(2)}, u32[]{:S(2)}) collective-permute-start(bf16[128,1024]{1,0:T(8,128)(2,1)S(1)} %collective-permute-done.5.refs_1_), channel_id=1, source_target_pairs={{0,8},{1,25},{2,10},{3,27},{4,12},{5,29},{6,14},{7,31},{8,0},{9,17... | collective-permute-start | bytes 786440 | tf_op jit(solution)/shard_map/ppermute | solution.py:36
  37.8 1.7 %collective-permute-start.8 = (f32[32,128]{1,0:T(8,128)S(1)}, f32[32,128]{1,0:T(8,128)S(1)}, u32[]{:S(2)}, u32[]{:S(2)}) collective-permute-start(f32[32,128]{1,0:T(8,128)S(1)} %get-tuple-element.48.rows), channel_id=1, source_target_pairs={{0,1},{1,0},{2,3},{3,2},{4,5},{5,4},{6,7},{7,6},{8,9},{9,8},{10,11... | collective-permute-start | bytes 49160 | tf_op jit(solution)/shard_map/ppermute | solution.py:36
where the time goes:
time: 72.4 us; the launch traced here: 72.2 us
  blocking collectives  40.8 us (56%)
  starting transfers between devices  15 us (21%)
  Pallas kernels  11.9 us (16%)
  waiting for transfers between devices  3.74 us (5%)
  between operations  0.73 us (1%)
    all_to_all x1, blocking collectives, body(): received = lax.all_to_all(sent, 'wide', 0, 0, tiled=True)  22.7 us
    all_to_all x2, blocking collectives, exchange(): lax.all_to_all(value, BOTH, 0, 0, axis_index_groups=groups, tiled=True)  18.2 us
    ppermute x9, starting transfers between devices, move(): return lax.ppermute(value, BOTH, pairs)  15 us
    pallas_call x9, Pallas kernels, call(): pl.pallas_call(kernel, out_shape=out_shape, in_specs=[pl.BlockSpec(memory...  11.9 us
    ppermute x9, waiting for transfers between devices, move(): return lax.ppermute(value, BOTH, pairs)  3.74 us
  transfers between devices with their start and end apart: 9, of which 3 were waited for; matrix products, arithmetic and copies ran while one was open for 0% of the time, Pallas kernels for 11%

commit v1 on v0

--- a/solution.py
+++ b/solution.py
@@ -46,6 +46,10 @@
 
 def across(z, y, x, core):
     return z, partner(y, core), x, core
+
+
+def ahead_across(z, y, x, core):
+    return z, partner(y, core), x + 1 - 2 * core, core
 
 
 def to_core(z, y, x, core):
@@ -258,6 +262,7 @@
     )
     blocks[1, 0] = move(blocks[0, 0], behind)
     blocks[3, 0], blocks[0, 0] = after((blocks[3, 0], blocks[0, 0]))
+    blocks[2, 1] = move(blocks[3, 0], ahead_across)
     blocks[2, 0] = move(blocks[3, 0], ahead)
     blocks[3, 1] = move(blocks[3, 0], across)
     both = (held(sources), other)
@@ -268,9 +273,6 @@
         if n == 1:
             blocks[1, 0], rows[0] = after((blocks[1, 0], rows[0]))
             blocks[1, 1] = move(blocks[1, 0], across)
-        if n == 2:
-            blocks[2, 0], rows[1] = after((blocks[2, 0], rows[1]))
-            blocks[2, 1] = move(blocks[2, 0], across)
         part, row, col = call(
             functools.partial(some_kernel, scale),
             (kept(count), f32(16, LANES), f32(len(slots), LANES)),

time: 72.4 us -> 71.5 us (0.988)
  blocking collectives: 40.8 us -> 42.8 us
  waiting for transfers between devices: 3.74 us -> 1.84 us
  starting transfers between devices: 15 us -> 14 us
    ppermute x9, waiting for transfers between devices: 3.74 us -> 1.84 us  [move(): return lax.ppermute(value, BOTH, pairs)]
    all_to_all x2, blocking collectives: 18.2 us -> 19.6 us  [exchange(): lax.all_to_all(value, BOTH, 0, 0, axis_index_groups=groups, tiled=True)]
    ppermute x9, starting transfers between devices: 15 us -> 14 us  [move(): return lax.ppermute(value, BOTH, pairs)]
where the time goes in v1:
time: 71.5 us; the launch traced here: 71.3 us
  blocking collectives  42.8 us (60%)
  starting transfers between devices  14 us (20%)
  Pallas kernels  11.9 us (17%)
  waiting for transfers between devices  1.84 us (3%)
  between operations  0.75 us (1%)
    all_to_all x1, blocking collectives, body(): received = lax.all_to_all(sent, 'wide', 0, 0, tiled=True)  23.2 us
    all_to_all x2, blocking collectives, exchange(): lax.all_to_all(value, BOTH, 0, 0, axis_index_groups=groups, tiled=True)  19.6 us
    ppermute x9, starting transfers between devices, move(): return lax.ppermute(value, BOTH, pairs)  14 us
    pallas_call x9, Pallas kernels, call(): pl.pallas_call(kernel, out_shape=out_shape, in_specs=[pl.BlockSpec(memory...  11.9 us
    ppermute x9, waiting for transfers between devices, move(): return lax.ppermute(value, BOTH, pairs)  1.84 us
  transfers between devices with their start and end apart: 9, of which 3 were waited for; matrix products, arithmetic and copies ran while one was open for 0% of the time, Pallas kernels for 11%

profile of v1, /device:TPU:1, one launch (start us, length us, event | category | flops | bytes accessed | tf_op | source)
XLA Modules:
  0.0 71.3 jit_solution(17229303489690534982)
XLA Ops:
  0.6 3.3 %collective-permute-start = (bf16[1024,1024]{1,0:T(8,128)(2,1)}, bf16[1024,1024]{1,0:T(8,128)(2,1)S(1)}, u32[]{:S(2)}, u32[]{:S(2)}) collective-permute-start(bf16[1024,1024]{1,0:T(8,128)(2,1)} %sources.1), channel_id=1, source_target_pairs={{0,1},{1,0},{2,3},{3,2},{4,5},{5,4},{6,7},{7,6},{8,9},{9,8},{10,11... | collective-permute-start | bytes 6291464 | tf_op jit(solution)/shard_map/ppermute | solution.py:36
  4.0 0.7 %collective-permute-start.1 = (bf16[128,1024]{1,0:T(8,128)(2,1)}, bf16[128,1024]{1,0:T(8,128)(2,1)S(1)}, u32[]{:S(2)}, u32[]{:S(2)}) collective-permute-start(bf16[128,1024]{1,0:T(8,128)(2,1)} %targets.1), channel_id=1, source_target_pairs={{0,2},{1,7},{2,4},{3,1},{4,6},{5,3},{6,0},{7,5},{8,10},{9,15},{10,... | collective-permute-start | bytes 786440 | tf_op jit(solution)/shard_map/ppermute | solution.py:36
  4.7 2.7 %collective-permute-start.2 = (bf16[128,1024]{1,0:T(8,128)(2,1)}, bf16[128,1024]{1,0:T(8,128)(2,1)S(1)}, u32[]{:S(2)}, u32[]{:S(2)}) collective-permute-start(bf16[128,1024]{1,0:T(8,128)(2,1)} %targets.1), channel_id=1, source_target_pairs={{0,8},{1,25},{2,10},{3,27},{4,12},{5,29},{6,14},{7,31},{8,0},{9,17... | collective-permute-start | bytes 786440 | tf_op jit(solution)/shard_map/ppermute | solution.py:36
  7.4 1.7 %shard_map.41 = (bf16[1024,1024]{1,0:T(8,128)(2,1)S(1)}, bf16[128,1024]{1,0:T(8,128)(2,1)S(1)}) custom-call(bf16[1024,1024]{1,0:T(8,128)(2,1)} %sources.1, bf16[128,1024]{1,0:T(8,128)(2,1)} %targets.1), custom_call_target="tpu_custom_call" | custom-call | bytes 2359296 | tf_op jit(solution)/shard_map/pallas_call | solution.py:83
  9.1 0.1 collective-permute-start.3
  9.2 0.5 collective-permute-done.1.refs_0_
  9.7 4.1 %collective-permute-start.7 = (bf16[128,1024]{1,0:T(8,128)(2,1)S(1)}, bf16[128,1024]{1,0:T(8,128)(2,1)S(1)}, u32[]{:S(2)}, u32[]{:S(2)}) collective-permute-start(bf16[128,1024]{1,0:T(8,128)(2,1)S(1)} %collective-permute-done.1.refs_0_), channel_id=1, source_target_pairs={{0,10},{1,31},{2,12},{3,25},{4,14},{5,27},{6,8},{7,29},{8,2},{9,23... | collective-permute-start | bytes 786440 | tf_op jit(solution)/shard_map/ppermute | solution.py:36
  13.8 0.0 collective-permute-start.5
  13.8 0.0 collective-permute-done.2.refs_1_
  13.8 0.5 collective-permute-start.4
  14.3 0.0 collective-permute-done.s1
  14.3 2.0 %shard_map.42 = (f32[256,2048]{1,0:T(8,128)S(1)}, f32[16,128]{1,0:T(8,128)S(1)}, f32[2,128]{1,0:T(2,128)S(1)}) custom-call(bf16[1024,1024]{1,0:T(8,128)(2,1)S(1)} %get-tuple-element.26.s0, bf16[1024,1024]{1,0:T(8,128)(2,1)S(1)} %collective-permute-done.s1, bf16[128,1024]{1,0:T(8,128)(2,1)S(1)} %get-tuple-element.28.refs_0_, ...), custom_call_target="tpu_custom_call" | custom-call | flops 1073741824 | bytes 4718592 | tf_op jit(solution)/shard_map/pallas_call | solution.py:83
  16.3 0.0 collective-permute-done.3.refs_1_
  16.3 2.5 %collective-permute-start.6 = (bf16[128,1024]{1,0:T(8,128)(2,1)S(1)}, bf16[128,1024]{1,0:T(8,128)(2,1)S(1)}, u32[]{:S(2)}, u32[]{:S(2)}) collective-permute-start(bf16[128,1024]{1,0:T(8,128)(2,1)S(1)} %collective-permute-done.3.refs_1_), channel_id=1, source_target_pairs={{0,8},{1,25},{2,10},{3,27},{4,12},{5,29},{6,14},{7,31},{8,0},{9,17... | collective-permute-start | bytes 786440 | tf_op jit(solution)/shard_map/ppermute | solution.py:36
  18.8 2.0 %shard_map.43 = (f32[256,2048]{1,0:T(8,128)S(1)}, f32[16,128]{1,0:T(8,128)S(1)}, f32[2,128]{1,0:T(2,128)S(1)}) custom-call(bf16[1024,1024]{1,0:T(8,128)(2,1)S(1)} %get-tuple-element.26.s0, bf16[1024,1024]{1,0:T(8,128)(2,1)S(1)} %collective-permute-done.s1, bf16[128,1024]{1,0:T(8,128)(2,1)S(1)} %collective-permute-done.1.refs_0_, ...), custom_call_target="tpu_custom_call" | custom-call | flops 1073741824 | bytes 4718592 | tf_op jit(solution)/shard_map/pallas_call | solution.py:83
  20.8 0.0 collective-permute-done.5.refs_1_
  20.8 0.0 collective-permute-done.4.refs_0_
  20.9 2.0 %shard_map.44 = (f32[256,2048]{1,0:T(8,128)S(1)}, f32[16,128]{1,0:T(8,128)S(1)}, f32[2,128]{1,0:T(2,128)S(1)}) custom-call(bf16[1024,1024]{1,0:T(8,128)(2,1)S(1)} %get-tuple-element.26.s0, bf16[1024,1024]{1,0:T(8,128)(2,1)S(1)} %collective-permute-done.s1, bf16[128,1024]{1,0:T(8,128)(2,1)S(1)} %collective-permute-done.4.refs_0_, ...), custom_call_target="tpu_custom_call" | custom-call | flops 1073741824 | bytes 4718592 | tf_op jit(solution)/shard_map/pallas_call | solution.py:83
  22.9 0.0 collective-permute-done.7.tb
  22.9 0.2 collective-permute-done.6.ta
  23.0 2.0 %shard_map.45 = (f32[256,2048]{1,0:T(8,128)S(1)}, f32[16,128]{1,0:T(8,128)S(1)}, f32[64,128]{1,0:T(8,128)S(1)}) custom-call(bf16[1024,1024]{1,0:T(8,128)(2,1)S(1)} %get-tuple-element.26.s0, bf16[1024,1024]{1,0:T(8,128)(2,1)S(1)} %collective-permute-done.s1, bf16[128,1024]{1,0:T(8,128)(2,1)S(1)} %collective-permute-done.6.ta, ...), custom_call_target="tpu_custom_call" | custom-call | flops 1073741824 | bytes 4746240 | tf_op jit(solution)/shard_map/pallas_call | solution.py:83
  25.1 11.0 %all_to_all.33 = f32[8,8,128]{2,1,0:T(8,128)S(1)} all-to-all(f32[8,8,128]{2,1,0:T(8,128)S(1)} %bitcast.13), channel_id=1, replica_groups={{0,2,4,6,8,10,12,14},{16,18,20,22,24,26,28,30},{1,3,5,7,25,27,29,31},{1..., dimensions={0} | all-to-all | bytes 65536 | tf_op jit(solution)/shard_map/all_to_all | solution.py:246
  36.1 0.8 %shard_map.46 = (f32[32,128]{1,0:T(8,128)S(1)}, f32[8,128]{1,0:T(8,128)S(1)}) custom-call(f32[256,2048]{1,0:T(8,128)S(1)} %get-tuple-element.29.a0, f32[256,2048]{1,0:T(8,128)S(1)} %get-tuple-element.33.a1, f32[256,2048]{1,0:T(8,128)S(1)} %get-tuple-element.34.a2, f32[256,2048]{1,0:T(8,128)S(1)} %get-tuple-element.41.a3, f32[64,128]{1,0:T(8,128)S(1)} %bitcast.12, ...), custom_call_target="tpu_custom_call" | custom-call | flops 4194304 | bytes 8429568 | tf_op jit(solution)/shard_map/pallas_call | solution.py:83
  36.9 0.1 collective-permute-start.8
  37.0 1.2 %collective-permute-done.8.incoming = f32[32,128]{1,0:T(8,128)S(1)} collective-permute-done((f32[32,128]{1,0:T(8,128)S(1)}, f32[32,128]{1,0:T(8,128)S(1)}, u32[]{:S(2)}, u32[]{:S(2)}) %collective-permute-start.8) | collective-permute-done | bytes 16416 | tf_op jit(solution)/shard_map/ppermute | solution.py:36
  38.2 23.2 %all_to_all.34 = f32[16,32,128]{2,1,0:T(8,128)S(1)} all-to-all(f32[16,32,128]{2,1,0:T(8,128)S(1)} %bitcast.11), channel_id=1, replica_groups=mesh['wide'=16,'narrow'=16] {'wide'}, dimensions={0} | all-to-all | bytes 524288 | tf_op jit(solution)/shard_map/all_to_all | solution.py:309
  61.4 0.7 %shard_map.48 = (f32[8,128]{1,0:T(8,128)S(1)}, f32[8,128]{1,0:T(8,128)S(1)}) custom-call(f32[256,2048]{1,0:T(8,128)S(1)} %get-tuple-element.29.a0, f32[256,2048]{1,0:T(8,128)S(1)} %get-tuple-element.33.a1, f32[256,2048]{1,0:T(8,128)S(1)} %get-tuple-element.34.a2, f32[256,2048]{1,0:T(8,128)S(1)} %get-tuple-element.41.a3, f32[512,128]{1,0:T(8,128)S(1)} %bitcast.10, ...), custom_call_target="tpu_custom_call" | custom-call | flops 4194304 | bytes 8654848 | tf_op jit(solution)/shard_map/pallas_call | solution.py:83
  62.2 8.6 %all_to_all.35 = f32[8,1,128]{2,1,0:T(1,128)S(1)} all-to-all(f32[8,1,128]{2,1,0:T(1,128)S(1)} %bitcast.15), channel_id=1, replica_groups={{0,2,4,6,8,10,12,14},{16,18,20,22,24,26,28,30},{1,3,5,7,25,27,29,31},{1..., dimensions={0} | all-to-all | bytes 8192 | tf_op jit(solution)/shard_map/all_to_all | solution.py:246
  70.7 0.6 shard_map.49
  (1 shorter events, 0.0 us)
Async XLA Ops:
  0.6 13.6 %collective-permute-start = (bf16[1024,1024]{1,0:T(8,128)(2,1)}, bf16[1024,1024]{1,0:T(8,128)(2,1)S(1)}, u32[]{:S(2)}, u32[]{:S(2)}) collective-permute-start(bf16[1024,1024]{1,0:T(8,128)(2,1)} %sources.1), channel_id=1, source_target_pairs={{0,1},{1,0},{2,3},{3,2},{4,5},{5,4},{6,7},{7,6},{8,9},{9,8},{10,11... | collective-permute-start | bytes 6291464 | tf_op jit(solution)/shard_map/ppermute | solution.py:36
  4.0 5.7 %collective-permute-start.1 = (bf16[128,1024]{1,0:T(8,128)(2,1)}, bf16[128,1024]{1,0:T(8,128)(2,1)S(1)}, u32[]{:S(2)}, u32[]{:S(2)}) collective-permute-start(bf16[128,1024]{1,0:T(8,128)(2,1)} %targets.1), channel_id=1, source_target_pairs={{0,2},{1,7},{2,4},{3,1},{4,6},{5,3},{6,0},{7,5},{8,10},{9,15},{10,... | collective-permute-start | bytes 786440 | tf_op jit(solution)/shard_map/ppermute | solution.py:36
  4.7 9.1 %collective-permute-start.2 = (bf16[128,1024]{1,0:T(8,128)(2,1)}, bf16[128,1024]{1,0:T(8,128)(2,1)S(1)}, u32[]{:S(2)}, u32[]{:S(2)}) collective-permute-start(bf16[128,1024]{1,0:T(8,128)(2,1)} %targets.1), channel_id=1, source_target_pairs={{0,8},{1,25},{2,10},{3,27},{4,12},{5,29},{6,14},{7,31},{8,0},{9,17... | collective-permute-start | bytes 786440 | tf_op jit(solution)/shard_map/ppermute | solution.py:36
  9.1 7.2 %collective-permute-start.3 = (bf16[128,1024]{1,0:T(8,128)(2,1)S(1)}, bf16[128,1024]{1,0:T(8,128)(2,1)S(1)}, u32[]{:S(2)}, u32[]{:S(2)}) collective-permute-start(bf16[128,1024]{1,0:T(8,128)(2,1)S(1)} %get-tuple-element.28.refs_0_), channel_id=1, source_target_pairs={{0,6},{1,3},{2,0},{3,5},{4,2},{5,7},{6,4},{7,1},{8,14},{9,11},{10,... | collective-permute-start | bytes 786440 | tf_op jit(solution)/shard_map/ppermute | solution.py:36
  9.7 13.2 %collective-permute-start.7 = (bf16[128,1024]{1,0:T(8,128)(2,1)S(1)}, bf16[128,1024]{1,0:T(8,128)(2,1)S(1)}, u32[]{:S(2)}, u32[]{:S(2)}) collective-permute-start(bf16[128,1024]{1,0:T(8,128)(2,1)S(1)} %collective-permute-done.1.refs_0_), channel_id=1, source_target_pairs={{0,10},{1,31},{2,12},{3,25},{4,14},{5,27},{6,8},{7,29},{8,2},{9,23... | collective-permute-start | bytes 786440 | tf_op jit(solution)/shard_map/ppermute | solution.py:36
  13.8 7.0 %collective-permute-start.5 = (bf16[128,1024]{1,0:T(8,128)(2,1)S(1)}, bf16[128,1024]{1,0:T(8,128)(2,1)S(1)}, u32[]{:S(2)}, u32[]{:S(2)}) collective-permute-start(bf16[128,1024]{1,0:T(8,128)(2,1)S(1)} %collective-permute-done.1.refs_0_), channel_id=1, source_target_pairs={{0,2},{1,7},{2,4},{3,1},{4,6},{5,3},{6,0},{7,5},{8,10},{9,15},{10,... | collective-permute-start | bytes 786440 | tf_op jit(solution)/shard_map/ppermute | solution.py:36
  13.8 7.0 %collective-permute-start.4 = (bf16[128,1024]{1,0:T(8,128)(2,1)S(1)}, bf16[128,1024]{1,0:T(8,128)(2,1)S(1)}, u32[]{:S(2)}, u32[]{:S(2)}) collective-permute-start(bf16[128,1024]{1,0:T(8,128)(2,1)S(1)} %collective-permute-done.1.refs_0_), channel_id=1, source_target_pairs={{0,8},{1,25},{2,10},{3,27},{4,12},{5,29},{6,14},{7,31},{8,0},{9,17... | collective-permute-start | bytes 786440 | tf_op jit(solution)/shard_map/ppermute | solution.py:36
  16.3 6.7 %collective-permute-start.6 = (bf16[128,1024]{1,0:T(8,128)(2,1)S(1)}, bf16[128,1024]{1,0:T(8,128)(2,1)S(1)}, u32[]{:S(2)}, u32[]{:S(2)}) collective-permute-start(bf16[128,1024]{1,0:T(8,128)(2,1)S(1)} %collective-permute-done.3.refs_1_), channel_id=1, source_target_pairs={{0,8},{1,25},{2,10},{3,27},{4,12},{5,29},{6,14},{7,31},{8,0},{9,17... | collective-permute-start | bytes 786440 | tf_op jit(solution)/shard_map/ppermute | solution.py:36
  36.9 1.3 %collective-permute-start.8 = (f32[32,128]{1,0:T(8,128)S(1)}, f32[32,128]{1,0:T(8,128)S(1)}, u32[]{:S(2)}, u32[]{:S(2)}) collective-permute-start(f32[32,128]{1,0:T(8,128)S(1)} %get-tuple-element.44.rows), channel_id=1, source_target_pairs={{0,1},{1,0},{2,3},{3,2},{4,5},{5,4},{6,7},{7,6},{8,9},{9,8},{10,11... | collective-permute-start | bytes 49160 | tf_op jit(solution)/shard_map/ppermute | solution.py:36

commit v2 on v1

--- a/solution.py
+++ b/solution.py
@@ -54,6 +54,10 @@
 
 def to_core(z, y, x, core):
     return z, y, x, 1 - core
+
+
+def to_far(z, y, x, core):
+    return z, y + 2, x, core
 
 
 def column_groups():
@@ -205,20 +209,25 @@
         rows[pl.ds(16 + j, 1), :] = jnp.max(best[j], axis=0, keepdims=True) * scale
 
 
-def join_kernel(rows, incoming, sent):
-    norm_own = log_sum([rows[:8], incoming[8:16]])
-    norm_other = log_sum([rows[8:16], incoming[:8]])
-    best_own = jnp.maximum(rows[16:24], incoming[24:])
-    best_other = jnp.maximum(rows[24:], incoming[16:24])
-    for e in range(16):
-        for k, value in enumerate((norm_own, norm_other, best_own, best_other)):
-            sent[pl.ds(e * 32 + k * 8, 8), :] = value
+def core_kernel(rows, core, joint):
+    joint[:8] = log_sum([rows[:8], core[8:16]])
+    joint[8:16] = log_sum([rows[8:16], core[:8]])
+    joint[16:24] = jnp.maximum(rows[16:24], core[24:])
+    joint[24:] = jnp.maximum(rows[24:], core[16:24])
+
+
+def join_kernel(rows, far, sent):
+    norm = log_sum([rows[:16], far[:16]])
+    best = jnp.maximum(rows[16:], far[16:])
+    for e in range(ZS):
+        sent[pl.ds(e * 32, 16), :] = norm
+        sent[pl.ds(e * 32 + 16, 16), :] = best
 
 
 def col_best_kernel(scale, a0, a1, a2, a3, received, col_norm, sent, row_best):
-    parts = [received[pl.ds(e * 32, 16), :] for e in range(16)]
+    parts = [received[pl.ds(e * 32, 16), :] for e in range(ZS)]
     row_norm = log_sum(parts)
-    best = functools.reduce(jnp.maximum, [received[pl.ds(e * 32 + 16, 8), :] for e in range(16)])
+    best = functools.reduce(jnp.maximum, [received[pl.ds(e * 32 + 16, 8), :] for e in range(ZS)])
     row_best[...] = best - 0.5 * row_norm[:8]
     place = own_place()
     norms = row_norm * (0.5 / scale)
@@ -305,8 +314,10 @@
         row_joint,
         flops=2 * 1024 * 2048,
     )
-    sent = call(join_kernel, f32(512, LANES), joint, move(joint, to_core))
-    received = lax.all_to_all(sent, "wide", 0, 0, tiled=True)
+    joint = call(core_kernel, f32(32, LANES), joint, move(joint, to_core))
+    sent = call(join_kernel, f32(ZS * 32, LANES), joint, move(joint, to_far))
+    along_z = [[2 * z + k for z in range(ZS)] for k in range(2)]
+    received = lax.all_to_all(sent, "wide", 0, 0, axis_index_groups=along_z, tiled=True)
     sent, row_best = call(
         functools.partial(col_best_kernel, scale),
         (f32(GROUP, LANES), pltpu.VMEM((8, LANES), jnp.float32)),

time: 71.5 us -> 69.8 us (0.976)
  blocking collectives: 42.8 us -> 36.9 us
  starting transfers between devices: 14 us -> 16.5 us
  waiting for transfers between devices: 1.84 us -> 3.55 us
    all_to_all x1, blocking collectives: 23.2 us -> 15.9 us  [body(): lax.all_to_all(sent, 'wide', 0, 0, axis_index_groups=along_z, tiled=True)]
    ppermute x9 -> x10, starting transfers between devices: 14 us -> 16.5 us  [move(): return lax.ppermute(value, BOTH, pairs)]
    ppermute x9 -> x10, waiting for transfers between devices: 1.84 us -> 3.55 us  [move(): return lax.ppermute(value, BOTH, pairs)]
    all_to_all x2, blocking collectives: 19.6 us -> 21 us  [exchange(): lax.all_to_all(value, BOTH, 0, 0, axis_index_groups=groups, tiled=True)]
    pallas_call x9 -> x10, Pallas kernels: 11.9 us -> 11.9 us  [call(): pl.pallas_call(kernel, out_shape=out_shape, in_specs=[pl.BlockSpec(memory...]
  transfers between devices with their start and end apart: 9 -> 10, of which waited for: 3 -> 4; matrix products, arithmetic and copies ran while one was open for 0% -> 0% of each run, Pallas kernels for 11% -> 11%
where the time goes in v2:
time: 69.8 us; the launch traced here: 69.6 us
  blocking collectives  36.9 us (53%)
  starting transfers between devices  16.5 us (24%)
  Pallas kernels  11.9 us (17%)
  waiting for transfers between devices  3.55 us (5%)
  between operations  0.74 us (1%)
    all_to_all x2, blocking collectives, exchange(): lax.all_to_all(value, BOTH, 0, 0, axis_index_groups=groups, tiled=True)  21 us
    ppermute x10, starting transfers between devices, move(): return lax.ppermute(value, BOTH, pairs)  16.5 us
    all_to_all x1, blocking collectives, body(): lax.all_to_all(sent, 'wide', 0, 0, axis_index_groups=along_z, tiled=True)  15.9 us
    pallas_call x10, Pallas kernels, call(): pl.pallas_call(kernel, out_shape=out_shape, in_specs=[pl.BlockSpec(memory...  11.9 us
    ppermute x10, waiting for transfers between devices, move(): return lax.ppermute(value, BOTH, pairs)  3.55 us
  transfers between devices with their start and end apart: 10, of which 4 were waited for; matrix products, arithmetic and copies ran while one was open for 0% of the time, Pallas kernels for 11%

profile of v2, /device:TPU:1, one launch (start us, length us, event | category | flops | bytes accessed | tf_op | source)
XLA Modules:
  0.0 69.6 jit_solution(13316468450514991756)
XLA Ops:
  0.6 3.3 %collective-permute-start = (bf16[1024,1024]{1,0:T(8,128)(2,1)}, bf16[1024,1024]{1,0:T(8,128)(2,1)S(1)}, u32[]{:S(2)}, u32[]{:S(2)}) collective-permute-start(bf16[1024,1024]{1,0:T(8,128)(2,1)} %sources.1), channel_id=1, source_target_pairs={{0,1},{1,0},{2,3},{3,2},{4,5},{5,4},{6,7},{7,6},{8,9},{9,8},{10,11... | collective-permute-start | bytes 6291464 | tf_op jit(solution)/shard_map/ppermute | solution.py:36
  4.0 0.7 %collective-permute-start.1 = (bf16[128,1024]{1,0:T(8,128)(2,1)}, bf16[128,1024]{1,0:T(8,128)(2,1)S(1)}, u32[]{:S(2)}, u32[]{:S(2)}) collective-permute-start(bf16[128,1024]{1,0:T(8,128)(2,1)} %targets.1), channel_id=1, source_target_pairs={{0,2},{1,7},{2,4},{3,1},{4,6},{5,3},{6,0},{7,5},{8,10},{9,15},{10,... | collective-permute-start | bytes 786440 | tf_op jit(solution)/shard_map/ppermute | solution.py:36
  4.7 2.7 %collective-permute-start.2 = (bf16[128,1024]{1,0:T(8,128)(2,1)}, bf16[128,1024]{1,0:T(8,128)(2,1)S(1)}, u32[]{:S(2)}, u32[]{:S(2)}) collective-permute-start(bf16[128,1024]{1,0:T(8,128)(2,1)} %targets.1), channel_id=1, source_target_pairs={{0,8},{1,25},{2,10},{3,27},{4,12},{5,29},{6,14},{7,31},{8,0},{9,17... | collective-permute-start | bytes 786440 | tf_op jit(solution)/shard_map/ppermute | solution.py:36
  7.4 1.7 %shard_map.41 = (bf16[1024,1024]{1,0:T(8,128)(2,1)S(1)}, bf16[128,1024]{1,0:T(8,128)(2,1)S(1)}) custom-call(bf16[1024,1024]{1,0:T(8,128)(2,1)} %sources.1, bf16[128,1024]{1,0:T(8,128)(2,1)} %targets.1), custom_call_target="tpu_custom_call" | custom-call | bytes 2359296 | tf_op jit(solution)/shard_map/pallas_call | solution.py:87
  9.1 0.1 collective-permute-start.3
  9.2 0.5 collective-permute-done.1.refs_0_
  9.7 4.1 %collective-permute-start.7 = (bf16[128,1024]{1,0:T(8,128)(2,1)S(1)}, bf16[128,1024]{1,0:T(8,128)(2,1)S(1)}, u32[]{:S(2)}, u32[]{:S(2)}) collective-permute-start(bf16[128,1024]{1,0:T(8,128)(2,1)S(1)} %collective-permute-done.1.refs_0_), channel_id=1, source_target_pairs={{0,10},{1,31},{2,12},{3,25},{4,14},{5,27},{6,8},{7,29},{8,2},{9,23... | collective-permute-start | bytes 786440 | tf_op jit(solution)/shard_map/ppermute | solution.py:36
  13.8 0.0 collective-permute-start.5
  13.8 0.0 collective-permute-done.2.refs_1_
  13.8 0.5 collective-permute-start.4
  14.3 0.0 collective-permute-done.s1
  14.3 2.0 %shard_map.42 = (f32[256,2048]{1,0:T(8,128)S(1)}, f32[16,128]{1,0:T(8,128)S(1)}, f32[2,128]{1,0:T(2,128)S(1)}) custom-call(bf16[1024,1024]{1,0:T(8,128)(2,1)S(1)} %get-tuple-element.26.s0, bf16[1024,1024]{1,0:T(8,128)(2,1)S(1)} %collective-permute-done.s1, bf16[128,1024]{1,0:T(8,128)(2,1)S(1)} %get-tuple-element.28.refs_0_, ...), custom_call_target="tpu_custom_call" | custom-call | flops 1073741824 | bytes 4718592 | tf_op jit(solution)/shard_map/pallas_call | solution.py:87
  16.3 0.0 collective-permute-done.3.refs_1_
  16.3 2.5 %collective-permute-start.6 = (bf16[128,1024]{1,0:T(8,128)(2,1)S(1)}, bf16[128,1024]{1,0:T(8,128)(2,1)S(1)}, u32[]{:S(2)}, u32[]{:S(2)}) collective-permute-start(bf16[128,1024]{1,0:T(8,128)(2,1)S(1)} %collective-permute-done.3.refs_1_), channel_id=1, source_target_pairs={{0,8},{1,25},{2,10},{3,27},{4,12},{5,29},{6,14},{7,31},{8,0},{9,17... | collective-permute-start | bytes 786440 | tf_op jit(solution)/shard_map/ppermute | solution.py:36
  18.8 2.0 %shard_map.43 = (f32[256,2048]{1,0:T(8,128)S(1)}, f32[16,128]{1,0:T(8,128)S(1)}, f32[2,128]{1,0:T(2,128)S(1)}) custom-call(bf16[1024,1024]{1,0:T(8,128)(2,1)S(1)} %get-tuple-element.26.s0, bf16[1024,1024]{1,0:T(8,128)(2,1)S(1)} %collective-permute-done.s1, bf16[128,1024]{1,0:T(8,128)(2,1)S(1)} %collective-permute-done.1.refs_0_, ...), custom_call_target="tpu_custom_call" | custom-call | flops 1073741824 | bytes 4718592 | tf_op jit(solution)/shard_map/pallas_call | solution.py:87
  20.8 0.0 collective-permute-done.5.refs_1_
  20.8 0.0 collective-permute-done.4.refs_0_
  20.9 2.0 %shard_map.44 = (f32[256,2048]{1,0:T(8,128)S(1)}, f32[16,128]{1,0:T(8,128)S(1)}, f32[2,128]{1,0:T(2,128)S(1)}) custom-call(bf16[1024,1024]{1,0:T(8,128)(2,1)S(1)} %get-tuple-element.26.s0, bf16[1024,1024]{1,0:T(8,128)(2,1)S(1)} %collective-permute-done.s1, bf16[128,1024]{1,0:T(8,128)(2,1)S(1)} %collective-permute-done.4.refs_0_, ...), custom_call_target="tpu_custom_call" | custom-call | flops 1073741824 | bytes 4718592 | tf_op jit(solution)/shard_map/pallas_call | solution.py:87
  22.9 0.0 collective-permute-done.7.tb
  22.9 0.2 collective-permute-done.6.ta
  23.0 2.0 %shard_map.45 = (f32[256,2048]{1,0:T(8,128)S(1)}, f32[16,128]{1,0:T(8,128)S(1)}, f32[64,128]{1,0:T(8,128)S(1)}) custom-call(bf16[1024,1024]{1,0:T(8,128)(2,1)S(1)} %get-tuple-element.26.s0, bf16[1024,1024]{1,0:T(8,128)(2,1)S(1)} %collective-permute-done.s1, bf16[128,1024]{1,0:T(8,128)(2,1)S(1)} %collective-permute-done.6.ta, ...), custom_call_target="tpu_custom_call" | custom-call | flops 1073741824 | bytes 4746240 | tf_op jit(solution)/shard_map/pallas_call | solution.py:87
  25.1 11.0 %all_to_all.33 = f32[8,8,128]{2,1,0:T(8,128)S(1)} all-to-all(f32[8,8,128]{2,1,0:T(8,128)S(1)} %bitcast.13), channel_id=1, replica_groups={{0,2,4,6,8,10,12,14},{16,18,20,22,24,26,28,30},{1,3,5,7,25,27,29,31},{1..., dimensions={0} | all-to-all | bytes 65536 | tf_op jit(solution)/shard_map/all_to_all | solution.py:255
  36.1 0.8 %shard_map.46 = (f32[32,128]{1,0:T(8,128)S(1)}, f32[8,128]{1,0:T(8,128)S(1)}) custom-call(f32[256,2048]{1,0:T(8,128)S(1)} %get-tuple-element.29.a0, f32[256,2048]{1,0:T(8,128)S(1)} %get-tuple-element.33.a1, f32[256,2048]{1,0:T(8,128)S(1)} %get-tuple-element.34.a2, f32[256,2048]{1,0:T(8,128)S(1)} %get-tuple-element.41.a3, f32[64,128]{1,0:T(8,128)S(1)} %bitcast.12, ...), custom_call_target="tpu_custom_call" | custom-call | flops 4194304 | bytes 8429568 | tf_op jit(solution)/shard_map/pallas_call | solution.py:87
  36.9 0.1 collective-permute-start.8
  37.0 1.2 %collective-permute-done.8.core = f32[32,128]{1,0:T(8,128)S(1)} collective-permute-done((f32[32,128]{1,0:T(8,128)S(1)}, f32[32,128]{1,0:T(8,128)S(1)}, u32[]{:S(2)}, u32[]{:S(2)}) %collective-permute-start.8) | collective-permute-done | bytes 16416 | tf_op jit(solution)/shard_map/ppermute | solution.py:36
  38.2 2.5 %collective-permute-start.9 = (f32[32,128]{1,0:T(8,128)S(1)}, f32[32,128]{1,0:T(8,128)S(1)}, u32[]{:S(2)}, u32[]{:S(2)}) collective-permute-start(f32[32,128]{1,0:T(8,128)S(1)} %shard_map.47.rows), channel_id=1, source_target_pairs={{0,16},{1,17},{2,18},{3,19},{4,20},{5,21},{6,22},{7,23},{8,24},{9,... | collective-permute-start | bytes 49160 | tf_op jit(solution)/shard_map/ppermute | solution.py:36
  40.7 1.7 %collective-permute-done.9.far = f32[32,128]{1,0:T(8,128)S(1)} collective-permute-done((f32[32,128]{1,0:T(8,128)S(1)}, f32[32,128]{1,0:T(8,128)S(1)}, u32[]{:S(2)}, u32[]{:S(2)}) %collective-permute-start.9) | collective-permute-done | bytes 16416 | tf_op jit(solution)/shard_map/ppermute | solution.py:36
  42.4 15.9 %all_to_all.34 = f32[8,32,128]{2,1,0:T(8,128)S(1)} all-to-all(f32[8,32,128]{2,1,0:T(8,128)S(1)} %bitcast.11), channel_id=1, replica_groups={{0,32,64,96,128,160,192,224},{16,48,80,112,144,176,208,240},{1,33,65,97..., dimensions={0} | all-to-all | bytes 262144 | tf_op jit(solution)/shard_map/all_to_all | solution.py:320
  58.3 0.7 %shard_map.49 = (f32[8,128]{1,0:T(8,128)S(1)}, f32[8,128]{1,0:T(8,128)S(1)}) custom-call(f32[256,2048]{1,0:T(8,128)S(1)} %get-tuple-element.29.a0, f32[256,2048]{1,0:T(8,128)S(1)} %get-tuple-element.33.a1, f32[256,2048]{1,0:T(8,128)S(1)} %get-tuple-element.34.a2, f32[256,2048]{1,0:T(8,128)S(1)} %get-tuple-element.41.a3, f32[256,128]{1,0:T(8,128)S(1)} %bitcast.10, ...), custom_call_target="tpu_custom_call" | custom-call | flops 4194304 | bytes 8523776 | tf_op jit(solution)/shard_map/pallas_call | solution.py:87
  59.0 9.9 %all_to_all.35 = f32[8,1,128]{2,1,0:T(1,128)S(1)} all-to-all(f32[8,1,128]{2,1,0:T(1,128)S(1)} %bitcast.15), channel_id=1, replica_groups={{0,2,4,6,8,10,12,14},{16,18,20,22,24,26,28,30},{1,3,5,7,25,27,29,31},{1..., dimensions={0} | all-to-all | bytes 8192 | tf_op jit(solution)/shard_map/all_to_all | solution.py:255
  69.0 0.6 shard_map.50
  (2 shorter events, 0.0 us)
Async XLA Ops:
  0.6 13.6 %collective-permute-start = (bf16[1024,1024]{1,0:T(8,128)(2,1)}, bf16[1024,1024]{1,0:T(8,128)(2,1)S(1)}, u32[]{:S(2)}, u32[]{:S(2)}) collective-permute-start(bf16[1024,1024]{1,0:T(8,128)(2,1)} %sources.1), channel_id=1, source_target_pairs={{0,1},{1,0},{2,3},{3,2},{4,5},{5,4},{6,7},{7,6},{8,9},{9,8},{10,11... | collective-permute-start | bytes 6291464 | tf_op jit(solution)/shard_map/ppermute | solution.py:36
  4.0 5.7 %collective-permute-start.1 = (bf16[128,1024]{1,0:T(8,128)(2,1)}, bf16[128,1024]{1,0:T(8,128)(2,1)S(1)}, u32[]{:S(2)}, u32[]{:S(2)}) collective-permute-start(bf16[128,1024]{1,0:T(8,128)(2,1)} %targets.1), channel_id=1, source_target_pairs={{0,2},{1,7},{2,4},{3,1},{4,6},{5,3},{6,0},{7,5},{8,10},{9,15},{10,... | collective-permute-start | bytes 786440 | tf_op jit(solution)/shard_map/ppermute | solution.py:36
  4.7 9.1 %collective-permute-start.2 = (bf16[128,1024]{1,0:T(8,128)(2,1)}, bf16[128,1024]{1,0:T(8,128)(2,1)S(1)}, u32[]{:S(2)}, u32[]{:S(2)}) collective-permute-start(bf16[128,1024]{1,0:T(8,128)(2,1)} %targets.1), channel_id=1, source_target_pairs={{0,8},{1,25},{2,10},{3,27},{4,12},{5,29},{6,14},{7,31},{8,0},{9,17... | collective-permute-start | bytes 786440 | tf_op jit(solution)/shard_map/ppermute | solution.py:36
  9.1 7.2 %collective-permute-start.3 = (bf16[128,1024]{1,0:T(8,128)(2,1)S(1)}, bf16[128,1024]{1,0:T(8,128)(2,1)S(1)}, u32[]{:S(2)}, u32[]{:S(2)}) collective-permute-start(bf16[128,1024]{1,0:T(8,128)(2,1)S(1)} %get-tuple-element.28.refs_0_), channel_id=1, source_target_pairs={{0,6},{1,3},{2,0},{3,5},{4,2},{5,7},{6,4},{7,1},{8,14},{9,11},{10,... | collective-permute-start | bytes 786440 | tf_op jit(solution)/shard_map/ppermute | solution.py:36
  9.7 13.2 %collective-permute-start.7 = (bf16[128,1024]{1,0:T(8,128)(2,1)S(1)}, bf16[128,1024]{1,0:T(8,128)(2,1)S(1)}, u32[]{:S(2)}, u32[]{:S(2)}) collective-permute-start(bf16[128,1024]{1,0:T(8,128)(2,1)S(1)} %collective-permute-done.1.refs_0_), channel_id=1, source_target_pairs={{0,10},{1,31},{2,12},{3,25},{4,14},{5,27},{6,8},{7,29},{8,2},{9,23... | collective-permute-start | bytes 786440 | tf_op jit(solution)/shard_map/ppermute | solution.py:36
  13.8 7.0 %collective-permute-start.5 = (bf16[128,1024]{1,0:T(8,128)(2,1)S(1)}, bf16[128,1024]{1,0:T(8,128)(2,1)S(1)}, u32[]{:S(2)}, u32[]{:S(2)}) collective-permute-start(bf16[128,1024]{1,0:T(8,128)(2,1)S(1)} %collective-permute-done.1.refs_0_), channel_id=1, source_target_pairs={{0,2},{1,7},{2,4},{3,1},{4,6},{5,3},{6,0},{7,5},{8,10},{9,15},{10,... | collective-permute-start | bytes 786440 | tf_op jit(solution)/shard_map/ppermute | solution.py:36
  13.8 7.0 %collective-permute-start.4 = (bf16[128,1024]{1,0:T(8,128)(2,1)S(1)}, bf16[128,1024]{1,0:T(8,128)(2,1)S(1)}, u32[]{:S(2)}, u32[]{:S(2)}) collective-permute-start(bf16[128,1024]{1,0:T(8,128)(2,1)S(1)} %collective-permute-done.1.refs_0_), channel_id=1, source_target_pairs={{0,8},{1,25},{2,10},{3,27},{4,12},{5,29},{6,14},{7,31},{8,0},{9,17... | collective-permute-start | bytes 786440 | tf_op jit(solution)/shard_map/ppermute | solution.py:36
  16.3 6.7 %collective-permute-start.6 = (bf16[128,1024]{1,0:T(8,128)(2,1)S(1)}, bf16[128,1024]{1,0:T(8,128)(2,1)S(1)}, u32[]{:S(2)}, u32[]{:S(2)}) collective-permute-start(bf16[128,1024]{1,0:T(8,128)(2,1)S(1)} %collective-permute-done.3.refs_1_), channel_id=1, source_target_pairs={{0,8},{1,25},{2,10},{3,27},{4,12},{5,29},{6,14},{7,31},{8,0},{9,17... | collective-permute-start | bytes 786440 | tf_op jit(solution)/shard_map/ppermute | solution.py:36
  36.9 1.3 %collective-permute-start.8 = (f32[32,128]{1,0:T(8,128)S(1)}, f32[32,128]{1,0:T(8,128)S(1)}, u32[]{:S(2)}, u32[]{:S(2)}) collective-permute-start(f32[32,128]{1,0:T(8,128)S(1)} %get-tuple-element.44.rows), channel_id=1, source_target_pairs={{0,1},{1,0},{2,3},{3,2},{4,5},{5,4},{6,7},{7,6},{8,9},{9,8},{10,11... | collective-permute-start | bytes 49160 | tf_op jit(solution)/shard_map/ppermute | solution.py:36
  38.2 4.2 %collective-permute-start.9 = (f32[32,128]{1,0:T(8,128)S(1)}, f32[32,128]{1,0:T(8,128)S(1)}, u32[]{:S(2)}, u32[]{:S(2)}) collective-permute-start(f32[32,128]{1,0:T(8,128)S(1)} %shard_map.47.rows), channel_id=1, source_target_pairs={{0,16},{1,17},{2,18},{3,19},{4,20},{5,21},{6,22},{7,23},{8,24},{9,... | collective-permute-start | bytes 49160 | tf_op jit(solution)/shard_map/ppermute | solution.py:36

commit v3 on v2

--- a/solution.py
+++ b/solution.py
@@ -123,7 +123,7 @@
     return ((y_lo + dy) % 2) * 4 + (x + 4 + dx * (1 - 2 * core)) % 4
 
 
-CALLS = (((0, 0), (0, 1)), ((3, 0), (1, 0)), ((3, 1), (2, 0)), ((1, 1), (2, 1)))
+CALLS = (((0, 0), (0, 1)), ((3, 0), (1, 0)), ((3, 1), (2, 0), (2, 1)), ((1, 1),))
 SLOTS = tuple((call, k, slot) for call, slots in enumerate(CALLS) for k, slot in enumerate(slots))
 
 
@@ -170,11 +170,10 @@
         col_part[pl.ds(k, 1), :] = row
 
 
-def end_kernel(scale, s0, s1, ta, tb, *refs):
+def end_kernel(scale, s0, s1, ta, *refs):
     rows, cols = refs[:3], refs[3:6]
     scores, joint, sent, scratch, last = refs[6:]
-    targets = jnp.concatenate([ta[...], tb[...]], axis=0)
-    ends = products(scale, s0, s1, targets, scores, last)
+    ends = products(scale, s0, s1, ta[...], scores, last)
     joint[...] = log_sum([row[...] for row in rows] + [last[...]])
     place = own_place()
     for call, k, slot in SLOTS:
@@ -212,22 +211,21 @@
 def core_kernel(rows, core, joint):
     joint[:8] = log_sum([rows[:8], core[8:16]])
     joint[8:16] = log_sum([rows[8:16], core[:8]])
-    joint[16:24] = jnp.maximum(rows[16:24], core[24:])
-    joint[24:] = jnp.maximum(rows[24:], core[16:24])
+    joint[16:] = jnp.maximum(rows[16:24], core[24:])
 
 
 def join_kernel(rows, far, sent):
     norm = log_sum([rows[:16], far[:16]])
     best = jnp.maximum(rows[16:], far[16:])
     for e in range(ZS):
-        sent[pl.ds(e * 32, 16), :] = norm
-        sent[pl.ds(e * 32 + 16, 16), :] = best
+        sent[pl.ds(e * 24, 16), :] = norm
+        sent[pl.ds(e * 24 + 16, 8), :] = best
 
 
 def col_best_kernel(scale, a0, a1, a2, a3, received, col_norm, sent, row_best):
-    parts = [received[pl.ds(e * 32, 16), :] for e in range(ZS)]
+    parts = [received[pl.ds(e * 24, 16), :] for e in range(ZS)]
     row_norm = log_sum(parts)
-    best = functools.reduce(jnp.maximum, [received[pl.ds(e * 32 + 16, 8), :] for e in range(ZS)])
+    best = functools.reduce(jnp.maximum, [received[pl.ds(e * 24 + 16, 8), :] for e in range(ZS)])
     row_best[...] = best - 0.5 * row_norm[:8]
     place = own_place()
     norms = row_norm * (0.5 / scale)
@@ -295,13 +293,13 @@
         cols.append(col)
     part, row_joint, sent = call(
         functools.partial(end_kernel, scale),
-        (kept(2 * LANES), f32(16, LANES), f32(GROUP * GROUP, LANES)),
+        (kept(LANES), f32(16, LANES), f32(GROUP * GROUP, LANES)),
         *both,
         *[blocks[slot] for slot in CALLS[-1]],
         *rows,
         *cols,
-        flops=4 * LANES * 2048 * 1024,
-        exps=4 * LANES * 2048,
+        flops=2 * LANES * 2048 * 1024,
+        exps=2 * LANES * 2048,
         scratch=[pltpu.VMEM((GROUP, LANES), jnp.float32), pltpu.VMEM((16, LANES), jnp.float32)],
     )
     scores.append(held(part))
@@ -314,8 +312,8 @@
         row_joint,
         flops=2 * 1024 * 2048,
     )
-    joint = call(core_kernel, f32(32, LANES), joint, move(joint, to_core))
-    sent = call(join_kernel, f32(ZS * 32, LANES), joint, move(joint, to_far))
+    joint = call(core_kernel, f32(24, LANES), joint, move(joint, to_core))
+    sent = call(join_kernel, f32(ZS * 24, LANES), joint, move(joint, to_far))
     along_z = [[2 * z + k for z in range(ZS)] for k in range(2)]
     received = lax.all_to_all(sent, "wide", 0, 0, axis_index_groups=along_z, tiled=True)
     sent, row_best = call(

time: 69.8 us -> 69.3 us (level)
  blocking collectives: 36.9 us -> 36 us
  transfers between devices with their start and end apart: 10 -> 10, of which waited for: 4 -> 3; matrix products, arithmetic and copies ran while one was open for 0% -> 0% of each run, Pallas kernels for 11% -> 12%
where the time goes in v3:
time: 69.3 us; the launch traced here: 69.1 us
  blocking collectives  36 us (52%)
  starting transfers between devices  16.5 us (24%)
  Pallas kernels  12.5 us (18%)
  waiting for transfers between devices  3.35 us (5%)
  between operations  0.74 us (1%)
    all_to_all x2, blocking collectives, exchange(): lax.all_to_all(value, BOTH, 0, 0, axis_index_groups=groups, tiled=True)  20.4 us
    ppermute x10, starting transfers between devices, move(): return lax.ppermute(value, BOTH, pairs)  16.5 us
    all_to_all x1, blocking collectives, body(): lax.all_to_all(sent, 'wide', 0, 0, axis_index_groups=along_z, tiled=True)  15.6 us
    pallas_call x10, Pallas kernels, call(): pl.pallas_call(kernel, out_shape=out_shape, in_specs=[pl.BlockSpec(memory...  12.5 us
    ppermute x10, waiting for transfers between devices, move(): return lax.ppermute(value, BOTH, pairs)  3.35 us
  transfers between devices with their start and end apart: 10, of which 3 were waited for; matrix products, arithmetic and copies ran while one was open for 0% of the time, Pallas kernels for 12%

profile of v3, /device:TPU:1, one launch (start us, length us, event | category | flops | bytes accessed | tf_op | source)
XLA Modules:
  0.0 69.1 jit_solution(2300548028361725581)
XLA Ops:
  0.6 3.3 %collective-permute-start = (bf16[1024,1024]{1,0:T(8,128)(2,1)}, bf16[1024,1024]{1,0:T(8,128)(2,1)S(1)}, u32[]{:S(2)}, u32[]{:S(2)}) collective-permute-start(bf16[1024,1024]{1,0:T(8,128)(2,1)} %sources.1), channel_id=1, source_target_pairs={{0,1},{1,0},{2,3},{3,2},{4,5},{5,4},{6,7},{7,6},{8,9},{9,8},{10,11... | collective-permute-start | bytes 6291464 | tf_op jit(solution)/shard_map/ppermute | solution.py:36
  4.0 0.7 %collective-permute-start.1 = (bf16[128,1024]{1,0:T(8,128)(2,1)}, bf16[128,1024]{1,0:T(8,128)(2,1)S(1)}, u32[]{:S(2)}, u32[]{:S(2)}) collective-permute-start(bf16[128,1024]{1,0:T(8,128)(2,1)} %targets.1), channel_id=1, source_target_pairs={{0,2},{1,7},{2,4},{3,1},{4,6},{5,3},{6,0},{7,5},{8,10},{9,15},{10,... | collective-permute-start | bytes 786440 | tf_op jit(solution)/shard_map/ppermute | solution.py:36
  4.7 2.7 %collective-permute-start.2 = (bf16[128,1024]{1,0:T(8,128)(2,1)}, bf16[128,1024]{1,0:T(8,128)(2,1)S(1)}, u32[]{:S(2)}, u32[]{:S(2)}) collective-permute-start(bf16[128,1024]{1,0:T(8,128)(2,1)} %targets.1), channel_id=1, source_target_pairs={{0,8},{1,25},{2,10},{3,27},{4,12},{5,29},{6,14},{7,31},{8,0},{9,17... | collective-permute-start | bytes 786440 | tf_op jit(solution)/shard_map/ppermute | solution.py:36
  7.4 1.7 %shard_map.41 = (bf16[1024,1024]{1,0:T(8,128)(2,1)S(1)}, bf16[128,1024]{1,0:T(8,128)(2,1)S(1)}) custom-call(bf16[1024,1024]{1,0:T(8,128)(2,1)} %sources.1, bf16[128,1024]{1,0:T(8,128)(2,1)} %targets.1), custom_call_target="tpu_custom_call" | custom-call | bytes 2359296 | tf_op jit(solution)/shard_map/pallas_call | solution.py:87
  9.1 0.1 collective-permute-start.3
  9.2 0.5 collective-permute-done.1.refs_0_
  9.7 4.1 %collective-permute-start.6 = (bf16[128,1024]{1,0:T(8,128)(2,1)S(1)}, bf16[128,1024]{1,0:T(8,128)(2,1)S(1)}, u32[]{:S(2)}, u32[]{:S(2)}) collective-permute-start(bf16[128,1024]{1,0:T(8,128)(2,1)S(1)} %collective-permute-done.1.refs_0_), channel_id=1, source_target_pairs={{0,10},{1,31},{2,12},{3,25},{4,14},{5,27},{6,8},{7,29},{8,2},{9,23... | collective-permute-start | bytes 786440 | tf_op jit(solution)/shard_map/ppermute | solution.py:36
  13.8 0.0 collective-permute-start.5
  13.8 0.0 collective-permute-done.2.refs_1_
  13.8 0.5 collective-permute-start.4
  14.3 0.0 collective-permute-done.s1
  14.3 2.0 %shard_map.42 = (f32[256,2048]{1,0:T(8,128)S(1)}, f32[16,128]{1,0:T(8,128)S(1)}, f32[2,128]{1,0:T(2,128)S(1)}) custom-call(bf16[1024,1024]{1,0:T(8,128)(2,1)S(1)} %get-tuple-element.26.s0, bf16[1024,1024]{1,0:T(8,128)(2,1)S(1)} %collective-permute-done.s1, bf16[128,1024]{1,0:T(8,128)(2,1)S(1)} %get-tuple-element.28.refs_0_, ...), custom_call_target="tpu_custom_call" | custom-call | flops 1073741824 | bytes 4718592 | tf_op jit(solution)/shard_map/pallas_call | solution.py:87
  16.3 0.0 collective-permute-done.3.refs_1_
  16.3 2.5 %collective-permute-start.7 = (bf16[128,1024]{1,0:T(8,128)(2,1)S(1)}, bf16[128,1024]{1,0:T(8,128)(2,1)S(1)}, u32[]{:S(2)}, u32[]{:S(2)}) collective-permute-start(bf16[128,1024]{1,0:T(8,128)(2,1)S(1)} %collective-permute-done.3.refs_1_), channel_id=1, source_target_pairs={{0,8},{1,25},{2,10},{3,27},{4,12},{5,29},{6,14},{7,31},{8,0},{9,17... | collective-permute-start | bytes 786440 | tf_op jit(solution)/shard_map/ppermute | solution.py:36
  18.8 2.0 %shard_map.43 = (f32[256,2048]{1,0:T(8,128)S(1)}, f32[16,128]{1,0:T(8,128)S(1)}, f32[2,128]{1,0:T(2,128)S(1)}) custom-call(bf16[1024,1024]{1,0:T(8,128)(2,1)S(1)} %get-tuple-element.26.s0, bf16[1024,1024]{1,0:T(8,128)(2,1)S(1)} %collective-permute-done.s1, bf16[128,1024]{1,0:T(8,128)(2,1)S(1)} %collective-permute-done.1.refs_0_, ...), custom_call_target="tpu_custom_call" | custom-call | flops 1073741824 | bytes 4718592 | tf_op jit(solution)/shard_map/pallas_call | solution.py:87
  20.8 0.0 collective-permute-done.6.refs_2_
  20.8 0.0 collective-permute-done.5.refs_1_
  20.8 0.0 collective-permute-done.4.refs_0_
  20.8 2.9 %shard_map.44 = (f32[384,2048]{1,0:T(8,128)S(1)}, f32[16,128]{1,0:T(8,128)S(1)}, f32[3,128]{1,0:T(4,128)S(1)}) custom-call(bf16[1024,1024]{1,0:T(8,128)(2,1)S(1)} %get-tuple-element.26.s0, bf16[1024,1024]{1,0:T(8,128)(2,1)S(1)} %collective-permute-done.s1, bf16[128,1024]{1,0:T(8,128)(2,1)S(1)} %collective-permute-done.4.refs_0_, ...), custom_call_target="tpu_custom_call" | custom-call | flops 1610612736 | bytes 4980736 | tf_op jit(solution)/shard_map/pallas_call | solution.py:87
  23.8 0.0 collective-permute-done.7.ta
  23.8 1.8 %shard_map.45 = (f32[128,2048]{1,0:T(8,128)S(1)}, f32[16,128]{1,0:T(8,128)S(1)}, f32[64,128]{1,0:T(8,128)S(1)}) custom-call(bf16[1024,1024]{1,0:T(8,128)(2,1)S(1)} %get-tuple-element.26.s0, bf16[1024,1024]{1,0:T(8,128)(2,1)S(1)} %collective-permute-done.s1, bf16[128,1024]{1,0:T(8,128)(2,1)S(1)} %collective-permute-done.7.ta, ...), custom_call_target="tpu_custom_call" | custom-call | flops 536870912 | bytes 4484608 | tf_op jit(solution)/shard_map/pallas_call | solution.py:87
  25.6 10.4 %all_to_all.33 = f32[8,8,128]{2,1,0:T(8,128)S(1)} all-to-all(f32[8,8,128]{2,1,0:T(8,128)S(1)} %bitcast.13), channel_id=1, replica_groups={{0,2,4,6,8,10,12,14},{16,18,20,22,24,26,28,30},{1,3,5,7,25,27,29,31},{1..., dimensions={0} | all-to-all | bytes 65536 | tf_op jit(solution)/shard_map/all_to_all | solution.py:253
  36.0 0.8 %shard_map.46 = (f32[32,128]{1,0:T(8,128)S(1)}, f32[8,128]{1,0:T(8,128)S(1)}) custom-call(f32[256,2048]{1,0:T(8,128)S(1)} %get-tuple-element.29.a0, f32[256,2048]{1,0:T(8,128)S(1)} %get-tuple-element.33.a1, f32[384,2048]{1,0:T(8,128)S(1)} %get-tuple-element.34.a2, f32[128,2048]{1,0:T(8,128)S(1)} %get-tuple-element.41.a3, f32[64,128]{1,0:T(8,128)S(1)} %bitcast.12, ...), custom_call_target="tpu_custom_call" | custom-call | flops 4194304 | bytes 8429568 | tf_op jit(solution)/shard_map/pallas_call | solution.py:87
  36.8 0.1 collective-permute-start.8
  36.9 1.2 %collective-permute-done.8.core = f32[32,128]{1,0:T(8,128)S(1)} collective-permute-done((f32[32,128]{1,0:T(8,128)S(1)}, f32[32,128]{1,0:T(8,128)S(1)}, u32[]{:S(2)}, u32[]{:S(2)}) %collective-permute-start.8) | collective-permute-done | bytes 16416 | tf_op jit(solution)/shard_map/ppermute | solution.py:36
  38.1 2.5 %collective-permute-start.9 = (f32[24,128]{1,0:T(8,128)S(1)}, f32[24,128]{1,0:T(8,128)S(1)}, u32[]{:S(2)}, u32[]{:S(2)}) collective-permute-start(f32[24,128]{1,0:T(8,128)S(1)} %shard_map.47.rows), channel_id=1, source_target_pairs={{0,16},{1,17},{2,18},{3,19},{4,20},{5,21},{6,22},{7,23},{8,24},{9,... | collective-permute-start | bytes 36872 | tf_op jit(solution)/shard_map/ppermute | solution.py:36
  40.6 1.7 %collective-permute-done.9.far = f32[24,128]{1,0:T(8,128)S(1)} collective-permute-done((f32[24,128]{1,0:T(8,128)S(1)}, f32[24,128]{1,0:T(8,128)S(1)}, u32[]{:S(2)}, u32[]{:S(2)}) %collective-permute-start.9) | collective-permute-done | bytes 12320 | tf_op jit(solution)/shard_map/ppermute | solution.py:36
  42.2 15.6 %all_to_all.34 = f32[8,24,128]{2,1,0:T(8,128)S(1)} all-to-all(f32[8,24,128]{2,1,0:T(8,128)S(1)} %bitcast.11), channel_id=1, replica_groups={{0,32,64,96,128,160,192,224},{16,48,80,112,144,176,208,240},{1,33,65,97..., dimensions={0} | all-to-all | bytes 196608 | tf_op jit(solution)/shard_map/all_to_all | solution.py:318
  57.8 0.7 %shard_map.49 = (f32[8,128]{1,0:T(8,128)S(1)}, f32[8,128]{1,0:T(8,128)S(1)}) custom-call(f32[256,2048]{1,0:T(8,128)S(1)} %get-tuple-element.29.a0, f32[256,2048]{1,0:T(8,128)S(1)} %get-tuple-element.33.a1, f32[384,2048]{1,0:T(8,128)S(1)} %get-tuple-element.34.a2, f32[128,2048]{1,0:T(8,128)S(1)} %get-tuple-element.41.a3, f32[192,128]{1,0:T(8,128)S(1)} %bitcast.10, ...), custom_call_target="tpu_custom_call" | custom-call | flops 4194304 | bytes 8491008 | tf_op jit(solution)/shard_map/pallas_call | solution.py:87
  58.5 10.0 %all_to_all.35 = f32[8,1,128]{2,1,0:T(1,128)S(1)} all-to-all(f32[8,1,128]{2,1,0:T(1,128)S(1)} %bitcast.15), channel_id=1, replica_groups={{0,2,4,6,8,10,12,14},{16,18,20,22,24,26,28,30},{1,3,5,7,25,27,29,31},{1..., dimensions={0} | all-to-all | bytes 8192 | tf_op jit(solution)/shard_map/all_to_all | solution.py:253
  68.5 0.6 shard_map.50
  (2 shorter events, 0.0 us)
Async XLA Ops:
  0.6 13.6 %collective-permute-start = (bf16[1024,1024]{1,0:T(8,128)(2,1)}, bf16[1024,1024]{1,0:T(8,128)(2,1)S(1)}, u32[]{:S(2)}, u32[]{:S(2)}) collective-permute-start(bf16[1024,1024]{1,0:T(8,128)(2,1)} %sources.1), channel_id=1, source_target_pairs={{0,1},{1,0},{2,3},{3,2},{4,5},{5,4},{6,7},{7,6},{8,9},{9,8},{10,11... | collective-permute-start | bytes 6291464 | tf_op jit(solution)/shard_map/ppermute | solution.py:36
  4.0 5.7 %collective-permute-start.1 = (bf16[128,1024]{1,0:T(8,128)(2,1)}, bf16[128,1024]{1,0:T(8,128)(2,1)S(1)}, u32[]{:S(2)}, u32[]{:S(2)}) collective-permute-start(bf16[128,1024]{1,0:T(8,128)(2,1)} %targets.1), channel_id=1, source_target_pairs={{0,2},{1,7},{2,4},{3,1},{4,6},{5,3},{6,0},{7,5},{8,10},{9,15},{10,... | collective-permute-start | bytes 786440 | tf_op jit(solution)/shard_map/ppermute | solution.py:36
  4.7 9.1 %collective-permute-start.2 = (bf16[128,1024]{1,0:T(8,128)(2,1)}, bf16[128,1024]{1,0:T(8,128)(2,1)S(1)}, u32[]{:S(2)}, u32[]{:S(2)}) collective-permute-start(bf16[128,1024]{1,0:T(8,128)(2,1)} %targets.1), channel_id=1, source_target_pairs={{0,8},{1,25},{2,10},{3,27},{4,12},{5,29},{6,14},{7,31},{8,0},{9,17... | collective-permute-start | bytes 786440 | tf_op jit(solution)/shard_map/ppermute | solution.py:36
  9.1 7.2 %collective-permute-start.3 = (bf16[128,1024]{1,0:T(8,128)(2,1)S(1)}, bf16[128,1024]{1,0:T(8,128)(2,1)S(1)}, u32[]{:S(2)}, u32[]{:S(2)}) collective-permute-start(bf16[128,1024]{1,0:T(8,128)(2,1)S(1)} %get-tuple-element.28.refs_0_), channel_id=1, source_target_pairs={{0,6},{1,3},{2,0},{3,5},{4,2},{5,7},{6,4},{7,1},{8,14},{9,11},{10,... | collective-permute-start | bytes 786440 | tf_op jit(solution)/shard_map/ppermute | solution.py:36
  9.7 11.1 %collective-permute-start.6 = (bf16[128,1024]{1,0:T(8,128)(2,1)S(1)}, bf16[128,1024]{1,0:T(8,128)(2,1)S(1)}, u32[]{:S(2)}, u32[]{:S(2)}) collective-permute-start(bf16[128,1024]{1,0:T(8,128)(2,1)S(1)} %collective-permute-done.1.refs_0_), channel_id=1, source_target_pairs={{0,10},{1,31},{2,12},{3,25},{4,14},{5,27},{6,8},{7,29},{8,2},{9,23... | collective-permute-start | bytes 786440 | tf_op jit(solution)/shard_map/ppermute | solution.py:36
  13.8 7.0 %collective-permute-start.5 = (bf16[128,1024]{1,0:T(8,128)(2,1)S(1)}, bf16[128,1024]{1,0:T(8,128)(2,1)S(1)}, u32[]{:S(2)}, u32[]{:S(2)}) collective-permute-start(bf16[128,1024]{1,0:T(8,128)(2,1)S(1)} %collective-permute-done.1.refs_0_), channel_id=1, source_target_pairs={{0,2},{1,7},{2,4},{3,1},{4,6},{5,3},{6,0},{7,5},{8,10},{9,15},{10,... | collective-permute-start | bytes 786440 | tf_op jit(solution)/shard_map/ppermute | solution.py:36
  13.8 7.0 %collective-permute-start.4 = (bf16[128,1024]{1,0:T(8,128)(2,1)S(1)}, bf16[128,1024]{1,0:T(8,128)(2,1)S(1)}, u32[]{:S(2)}, u32[]{:S(2)}) collective-permute-start(bf16[128,1024]{1,0:T(8,128)(2,1)S(1)} %collective-permute-done.1.refs_0_), channel_id=1, source_target_pairs={{0,8},{1,25},{2,10},{3,27},{4,12},{5,29},{6,14},{7,31},{8,0},{9,17... | collective-permute-start | bytes 786440 | tf_op jit(solution)/shard_map/ppermute | solution.py:36
  16.3 7.5 %collective-permute-start.7 = (bf16[128,1024]{1,0:T(8,128)(2,1)S(1)}, bf16[128,1024]{1,0:T(8,128)(2,1)S(1)}, u32[]{:S(2)}, u32[]{:S(2)}) collective-permute-start(bf16[128,1024]{1,0:T(8,128)(2,1)S(1)} %collective-permute-done.3.refs_1_), channel_id=1, source_target_pairs={{0,8},{1,25},{2,10},{3,27},{4,12},{5,29},{6,14},{7,31},{8,0},{9,17... | collective-permute-start | bytes 786440 | tf_op jit(solution)/shard_map/ppermute | solution.py:36
  36.8 1.3 %collective-permute-start.8 = (f32[32,128]{1,0:T(8,128)S(1)}, f32[32,128]{1,0:T(8,128)S(1)}, u32[]{:S(2)}, u32[]{:S(2)}) collective-permute-start(f32[32,128]{1,0:T(8,128)S(1)} %get-tuple-element.44.rows), channel_id=1, source_target_pairs={{0,1},{1,0},{2,3},{3,2},{4,5},{5,4},{6,7},{7,6},{8,9},{9,8},{10,11... | collective-permute-start | bytes 49160 | tf_op jit(solution)/shard_map/ppermute | solution.py:36
  38.1 4.1 %collective-permute-start.9 = (f32[24,128]{1,0:T(8,128)S(1)}, f32[24,128]{1,0:T(8,128)S(1)}, u32[]{:S(2)}, u32[]{:S(2)}) collective-permute-start(f32[24,128]{1,0:T(8,128)S(1)} %shard_map.47.rows), channel_id=1, source_target_pairs={{0,16},{1,17},{2,18},{3,19},{4,20},{5,21},{6,22},{7,23},{8,24},{9,... | collective-permute-start | bytes 36872 | tf_op jit(solution)/shard_map/ppermute | solution.py:36

commit v4 on v3

--- a/solution.py
+++ b/solution.py
@@ -123,7 +123,7 @@
     return ((y_lo + dy) % 2) * 4 + (x + 4 + dx * (1 - 2 * core)) % 4
 
 
-CALLS = (((0, 0), (0, 1)), ((3, 0), (1, 0)), ((3, 1), (2, 0), (2, 1)), ((1, 1),))
+CALLS = (((0, 0), (0, 1)), ((3, 0), (1, 0)), ((2, 1), (3, 1), (2, 0)), ((1, 1),))
 SLOTS = tuple((call, k, slot) for call, slots in enumerate(CALLS) for k, slot in enumerate(slots))
 
 
@@ -269,9 +269,9 @@
     )
     blocks[1, 0] = move(blocks[0, 0], behind)
     blocks[3, 0], blocks[0, 0] = after((blocks[3, 0], blocks[0, 0]))
+    blocks[3, 1] = move(blocks[3, 0], across)
+    blocks[2, 0] = move(blocks[3, 0], ahead)
     blocks[2, 1] = move(blocks[3, 0], ahead_across)
-    blocks[2, 0] = move(blocks[3, 0], ahead)
-    blocks[3, 1] = move(blocks[3, 0], across)
     both = (held(sources), other)
 
     scores, rows, cols = [], [], []

time: 69.3 us -> 69.3 us (level)
  starting transfers between devices: 16.5 us -> 17.7 us
  blocking collectives: 36 us -> 34.9 us
    ppermute x10, starting transfers between devices: 16.5 us -> 17.7 us  [move(): return lax.ppermute(value, BOTH, pairs)]
    all_to_all x2, blocking collectives: 20.4 us -> 19.4 us  [exchange(): lax.all_to_all(value, BOTH, 0, 0, axis_index_groups=groups, tiled=True)]
  transfers between devices with their start and end apart: 10 -> 10, of which waited for: 3 -> 4; matrix products, arithmetic and copies ran while one was open for 0% -> 0% of each run, Pallas kernels for 12% -> 12%
where the time goes in v4:
time: 69.3 us; the launch traced here: 69.1 us
  blocking collectives  34.9 us (50%)
  starting transfers between devices  17.7 us (26%)
  Pallas kernels  12.5 us (18%)
  waiting for transfers between devices  3.21 us (5%)
  between operations  0.73 us (1%)
    all_to_all x2, blocking collectives, exchange(): lax.all_to_all(value, BOTH, 0, 0, axis_index_groups=groups, tiled=True)  19.4 us
    ppermute x10, starting transfers between devices, move(): return lax.ppermute(value, BOTH, pairs)  17.7 us
    all_to_all x1, blocking collectives, body(): lax.all_to_all(sent, 'wide', 0, 0, axis_index_groups=along_z, tiled=True)  15.5 us
    pallas_call x10, Pallas kernels, call(): pl.pallas_call(kernel, out_shape=out_shape, in_specs=[pl.BlockSpec(memory...  12.5 us
    ppermute x10, waiting for transfers between devices, move(): return lax.ppermute(value, BOTH, pairs)  3.21 us
  transfers between devices with their start and end apart: 10, of which 4 were waited for; matrix products, arithmetic and copies ran while one was open for 0% of the time, Pallas kernels for 12%

profile of v4, /device:TPU:1, one launch (start us, length us, event | category | flops | bytes accessed | tf_op | source)
XLA Modules:
  0.0 69.1 jit_solution(12116670902604399226)
XLA Ops:
  0.6 3.3 %collective-permute-start = (bf16[1024,1024]{1,0:T(8,128)(2,1)}, bf16[1024,1024]{1,0:T(8,128)(2,1)S(1)}, u32[]{:S(2)}, u32[]{:S(2)}) collective-permute-start(bf16[1024,1024]{1,0:T(8,128)(2,1)} %sources.1), channel_id=1, source_target_pairs={{0,1},{1,0},{2,3},{3,2},{4,5},{5,4},{6,7},{7,6},{8,9},{9,8},{10,11... | collective-permute-start | bytes 6291464 | tf_op jit(solution)/shard_map/ppermute | solution.py:36
  4.0 0.7 %collective-permute-start.1 = (bf16[128,1024]{1,0:T(8,128)(2,1)}, bf16[128,1024]{1,0:T(8,128)(2,1)S(1)}, u32[]{:S(2)}, u32[]{:S(2)}) collective-permute-start(bf16[128,1024]{1,0:T(8,128)(2,1)} %targets.1), channel_id=1, source_target_pairs={{0,2},{1,7},{2,4},{3,1},{4,6},{5,3},{6,0},{7,5},{8,10},{9,15},{10,... | collective-permute-start | bytes 786440 | tf_op jit(solution)/shard_map/ppermute | solution.py:36
  4.7 2.7 %collective-permute-start.2 = (bf16[128,1024]{1,0:T(8,128)(2,1)}, bf16[128,1024]{1,0:T(8,128)(2,1)S(1)}, u32[]{:S(2)}, u32[]{:S(2)}) collective-permute-start(bf16[128,1024]{1,0:T(8,128)(2,1)} %targets.1), channel_id=1, source_target_pairs={{0,8},{1,25},{2,10},{3,27},{4,12},{5,29},{6,14},{7,31},{8,0},{9,17... | collective-permute-start | bytes 786440 | tf_op jit(solution)/shard_map/ppermute | solution.py:36
  7.4 1.7 %shard_map.41 = (bf16[1024,1024]{1,0:T(8,128)(2,1)S(1)}, bf16[128,1024]{1,0:T(8,128)(2,1)S(1)}) custom-call(bf16[1024,1024]{1,0:T(8,128)(2,1)} %sources.1, bf16[128,1024]{1,0:T(8,128)(2,1)} %targets.1), custom_call_target="tpu_custom_call" | custom-call | bytes 2359296 | tf_op jit(solution)/shard_map/pallas_call | solution.py:87
  9.1 0.1 collective-permute-start.3
  9.2 0.5 collective-permute-done.1.refs_0_
  9.7 2.2 %collective-permute-start.6 = (bf16[128,1024]{1,0:T(8,128)(2,1)S(1)}, bf16[128,1024]{1,0:T(8,128)(2,1)S(1)}, u32[]{:S(2)}, u32[]{:S(2)}) collective-permute-start(bf16[128,1024]{1,0:T(8,128)(2,1)S(1)} %collective-permute-done.1.refs_0_), channel_id=1, source_target_pairs={{0,2},{1,7},{2,4},{3,1},{4,6},{5,3},{6,0},{7,5},{8,10},{9,15},{10,... | collective-permute-start | bytes 786440 | tf_op jit(solution)/shard_map/ppermute | solution.py:36
  11.9 2.2 %collective-permute-start.5 = (bf16[128,1024]{1,0:T(8,128)(2,1)S(1)}, bf16[128,1024]{1,0:T(8,128)(2,1)S(1)}, u32[]{:S(2)}, u32[]{:S(2)}) collective-permute-start(bf16[128,1024]{1,0:T(8,128)(2,1)S(1)} %collective-permute-done.1.refs_0_), channel_id=1, source_target_pairs={{0,8},{1,25},{2,10},{3,27},{4,12},{5,29},{6,14},{7,31},{8,0},{9,17... | collective-permute-start | bytes 786440 | tf_op jit(solution)/shard_map/ppermute | solution.py:36
  14.1 0.0 collective-permute-done.2.refs_1_
  14.1 0.6 collective-permute-start.4
  14.6 0.0 collective-permute-done.s1
  14.6 2.0 %shard_map.42 = (f32[256,2048]{1,0:T(8,128)S(1)}, f32[16,128]{1,0:T(8,128)S(1)}, f32[2,128]{1,0:T(2,128)S(1)}) custom-call(bf16[1024,1024]{1,0:T(8,128)(2,1)S(1)} %get-tuple-element.26.s0, bf16[1024,1024]{1,0:T(8,128)(2,1)S(1)} %collective-permute-done.s1, bf16[128,1024]{1,0:T(8,128)(2,1)S(1)} %get-tuple-element.28.refs_0_, ...), custom_call_target="tpu_custom_call" | custom-call | flops 1073741824 | bytes 4718592 | tf_op jit(solution)/shard_map/pallas_call | solution.py:87
  16.7 0.0 collective-permute-done.3.refs_1_
  16.7 2.1 %collective-permute-start.7 = (bf16[128,1024]{1,0:T(8,128)(2,1)S(1)}, bf16[128,1024]{1,0:T(8,128)(2,1)S(1)}, u32[]{:S(2)}, u32[]{:S(2)}) collective-permute-start(bf16[128,1024]{1,0:T(8,128)(2,1)S(1)} %collective-permute-done.3.refs_1_), channel_id=1, source_target_pairs={{0,8},{1,25},{2,10},{3,27},{4,12},{5,29},{6,14},{7,31},{8,0},{9,17... | collective-permute-start | bytes 786440 | tf_op jit(solution)/shard_map/ppermute | solution.py:36
  18.8 2.0 %shard_map.43 = (f32[256,2048]{1,0:T(8,128)S(1)}, f32[16,128]{1,0:T(8,128)S(1)}, f32[2,128]{1,0:T(2,128)S(1)}) custom-call(bf16[1024,1024]{1,0:T(8,128)(2,1)S(1)} %get-tuple-element.26.s0, bf16[1024,1024]{1,0:T(8,128)(2,1)S(1)} %collective-permute-done.s1, bf16[128,1024]{1,0:T(8,128)(2,1)S(1)} %collective-permute-done.1.refs_0_, ...), custom_call_target="tpu_custom_call" | custom-call | flops 1073741824 | bytes 4718592 | tf_op jit(solution)/shard_map/pallas_call | solution.py:87
  20.8 0.0 collective-permute-done.6.refs_2_
  20.8 0.0 collective-permute-done.5.refs_1_
  20.8 0.7 %collective-permute-done.4.refs_0_ = bf16[128,1024]{1,0:T(8,128)(2,1)S(1)} collective-permute-done((bf16[128,1024]{1,0:T(8,128)(2,1)S(1)}, bf16[128,1024]{1,0:T(8,128)(2,1)S(1)}, u32[]{:S(2)}, u32[]{:S(2)}) %collective-permute-start.4) | collective-permute-done | bytes 262176 | tf_op jit(solution)/shard_map/ppermute | solution.py:36
  21.5 2.9 %shard_map.44 = (f32[384,2048]{1,0:T(8,128)S(1)}, f32[16,128]{1,0:T(8,128)S(1)}, f32[3,128]{1,0:T(4,128)S(1)}) custom-call(bf16[1024,1024]{1,0:T(8,128)(2,1)S(1)} %get-tuple-element.26.s0, bf16[1024,1024]{1,0:T(8,128)(2,1)S(1)} %collective-permute-done.s1, bf16[128,1024]{1,0:T(8,128)(2,1)S(1)} %collective-permute-done.4.refs_0_, ...), custom_call_target="tpu_custom_call" | custom-call | flops 1610612736 | bytes 4980736 | tf_op jit(solution)/shard_map/pallas_call | solution.py:87
  24.4 0.0 collective-permute-done.7.ta
  24.5 1.8 %shard_map.45 = (f32[128,2048]{1,0:T(8,128)S(1)}, f32[16,128]{1,0:T(8,128)S(1)}, f32[64,128]{1,0:T(8,128)S(1)}) custom-call(bf16[1024,1024]{1,0:T(8,128)(2,1)S(1)} %get-tuple-element.26.s0, bf16[1024,1024]{1,0:T(8,128)(2,1)S(1)} %collective-permute-done.s1, bf16[128,1024]{1,0:T(8,128)(2,1)S(1)} %collective-permute-done.7.ta, ...), custom_call_target="tpu_custom_call" | custom-call | flops 536870912 | bytes 4484608 | tf_op jit(solution)/shard_map/pallas_call | solution.py:87
  26.3 9.4 %all_to_all.33 = f32[8,8,128]{2,1,0:T(8,128)S(1)} all-to-all(f32[8,8,128]{2,1,0:T(8,128)S(1)} %bitcast.13), channel_id=1, replica_groups={{0,2,4,6,8,10,12,14},{16,18,20,22,24,26,28,30},{1,3,5,7,25,27,29,31},{1..., dimensions={0} | all-to-all | bytes 65536 | tf_op jit(solution)/shard_map/all_to_all | solution.py:253
  35.6 0.8 %shard_map.46 = (f32[32,128]{1,0:T(8,128)S(1)}, f32[8,128]{1,0:T(8,128)S(1)}) custom-call(f32[256,2048]{1,0:T(8,128)S(1)} %get-tuple-element.29.a0, f32[256,2048]{1,0:T(8,128)S(1)} %get-tuple-element.33.a1, f32[384,2048]{1,0:T(8,128)S(1)} %get-tuple-element.34.a2, f32[128,2048]{1,0:T(8,128)S(1)} %get-tuple-element.41.a3, f32[64,128]{1,0:T(8,128)S(1)} %bitcast.12, ...), custom_call_target="tpu_custom_call" | custom-call | flops 4194304 | bytes 8429568 | tf_op jit(solution)/shard_map/pallas_call | solution.py:87
  36.4 0.8 %collective-permute-start.8 = (f32[32,128]{1,0:T(8,128)S(1)}, f32[32,128]{1,0:T(8,128)S(1)}, u32[]{:S(2)}, u32[]{:S(2)}) collective-permute-start(f32[32,128]{1,0:T(8,128)S(1)} %get-tuple-element.44.rows), channel_id=1, source_target_pairs={{0,1},{1,0},{2,3},{3,2},{4,5},{5,4},{6,7},{7,6},{8,9},{9,8},{10,11... | collective-permute-start | bytes 49160 | tf_op jit(solution)/shard_map/ppermute | solution.py:36
  37.2 0.8 %collective-permute-done.8.core = f32[32,128]{1,0:T(8,128)S(1)} collective-permute-done((f32[32,128]{1,0:T(8,128)S(1)}, f32[32,128]{1,0:T(8,128)S(1)}, u32[]{:S(2)}, u32[]{:S(2)}) %collective-permute-start.8) | collective-permute-done | bytes 16416 | tf_op jit(solution)/shard_map/ppermute | solution.py:36
  38.1 3.0 %collective-permute-start.9 = (f32[24,128]{1,0:T(8,128)S(1)}, f32[24,128]{1,0:T(8,128)S(1)}, u32[]{:S(2)}, u32[]{:S(2)}) collective-permute-start(f32[24,128]{1,0:T(8,128)S(1)} %shard_map.47.rows), channel_id=1, source_target_pairs={{0,16},{1,17},{2,18},{3,19},{4,20},{5,21},{6,22},{7,23},{8,24},{9,... | collective-permute-start | bytes 36872 | tf_op jit(solution)/shard_map/ppermute | solution.py:36
  41.0 1.2 %collective-permute-done.9.far = f32[24,128]{1,0:T(8,128)S(1)} collective-permute-done((f32[24,128]{1,0:T(8,128)S(1)}, f32[24,128]{1,0:T(8,128)S(1)}, u32[]{:S(2)}, u32[]{:S(2)}) %collective-permute-start.9) | collective-permute-done | bytes 12320 | tf_op jit(solution)/shard_map/ppermute | solution.py:36
  42.2 15.5 %all_to_all.34 = f32[8,24,128]{2,1,0:T(8,128)S(1)} all-to-all(f32[8,24,128]{2,1,0:T(8,128)S(1)} %bitcast.11), channel_id=1, replica_groups={{0,32,64,96,128,160,192,224},{16,48,80,112,144,176,208,240},{1,33,65,97..., dimensions={0} | all-to-all | bytes 196608 | tf_op jit(solution)/shard_map/all_to_all | solution.py:318
  57.7 0.7 %shard_map.49 = (f32[8,128]{1,0:T(8,128)S(1)}, f32[8,128]{1,0:T(8,128)S(1)}) custom-call(f32[256,2048]{1,0:T(8,128)S(1)} %get-tuple-element.29.a0, f32[256,2048]{1,0:T(8,128)S(1)} %get-tuple-element.33.a1, f32[384,2048]{1,0:T(8,128)S(1)} %get-tuple-element.34.a2, f32[128,2048]{1,0:T(8,128)S(1)} %get-tuple-element.41.a3, f32[192,128]{1,0:T(8,128)S(1)} %bitcast.10, ...), custom_call_target="tpu_custom_call" | custom-call | flops 4194304 | bytes 8491008 | tf_op jit(solution)/shard_map/pallas_call | solution.py:87
  58.4 10.1 %all_to_all.35 = f32[8,1,128]{2,1,0:T(1,128)S(1)} all-to-all(f32[8,1,128]{2,1,0:T(1,128)S(1)} %bitcast.15), channel_id=1, replica_groups={{0,2,4,6,8,10,12,14},{16,18,20,22,24,26,28,30},{1,3,5,7,25,27,29,31},{1..., dimensions={0} | all-to-all | bytes 8192 | tf_op jit(solution)/shard_map/all_to_all | solution.py:253
  68.5 0.6 shard_map.50
  (2 shorter events, 0.0 us)
Async XLA Ops:
  0.6 14.0 %collective-permute-start = (bf16[1024,1024]{1,0:T(8,128)(2,1)}, bf16[1024,1024]{1,0:T(8,128)(2,1)S(1)}, u32[]{:S(2)}, u32[]{:S(2)}) collective-permute-start(bf16[1024,1024]{1,0:T(8,128)(2,1)} %sources.1), channel_id=1, source_target_pairs={{0,1},{1,0},{2,3},{3,2},{4,5},{5,4},{6,7},{7,6},{8,9},{9,8},{10,11... | collective-permute-start | bytes 6291464 | tf_op jit(solution)/shard_map/ppermute | solution.py:36
  4.0 5.7 %collective-permute-start.1 = (bf16[128,1024]{1,0:T(8,128)(2,1)}, bf16[128,1024]{1,0:T(8,128)(2,1)S(1)}, u32[]{:S(2)}, u32[]{:S(2)}) collective-permute-start(bf16[128,1024]{1,0:T(8,128)(2,1)} %targets.1), channel_id=1, source_target_pairs={{0,2},{1,7},{2,4},{3,1},{4,6},{5,3},{6,0},{7,5},{8,10},{9,15},{10,... | collective-permute-start | bytes 786440 | tf_op jit(solution)/shard_map/ppermute | solution.py:36
  4.7 9.4 %collective-permute-start.2 = (bf16[128,1024]{1,0:T(8,128)(2,1)}, bf16[128,1024]{1,0:T(8,128)(2,1)S(1)}, u32[]{:S(2)}, u32[]{:S(2)}) collective-permute-start(bf16[128,1024]{1,0:T(8,128)(2,1)} %targets.1), channel_id=1, source_target_pairs={{0,8},{1,25},{2,10},{3,27},{4,12},{5,29},{6,14},{7,31},{8,0},{9,17... | collective-permute-start | bytes 786440 | tf_op jit(solution)/shard_map/ppermute | solution.py:36
  9.1 7.6 %collective-permute-start.3 = (bf16[128,1024]{1,0:T(8,128)(2,1)S(1)}, bf16[128,1024]{1,0:T(8,128)(2,1)S(1)}, u32[]{:S(2)}, u32[]{:S(2)}) collective-permute-start(bf16[128,1024]{1,0:T(8,128)(2,1)S(1)} %get-tuple-element.28.refs_0_), channel_id=1, source_target_pairs={{0,6},{1,3},{2,0},{3,5},{4,2},{5,7},{6,4},{7,1},{8,14},{9,11},{10,... | collective-permute-start | bytes 786440 | tf_op jit(solution)/shard_map/ppermute | solution.py:36
  9.7 11.1 %collective-permute-start.6 = (bf16[128,1024]{1,0:T(8,128)(2,1)S(1)}, bf16[128,1024]{1,0:T(8,128)(2,1)S(1)}, u32[]{:S(2)}, u32[]{:S(2)}) collective-permute-start(bf16[128,1024]{1,0:T(8,128)(2,1)S(1)} %collective-permute-done.1.refs_0_), channel_id=1, source_target_pairs={{0,2},{1,7},{2,4},{3,1},{4,6},{5,3},{6,0},{7,5},{8,10},{9,15},{10,... | collective-permute-start | bytes 786440 | tf_op jit(solution)/shard_map/ppermute | solution.py:36
  11.9 8.9 %collective-permute-start.5 = (bf16[128,1024]{1,0:T(8,128)(2,1)S(1)}, bf16[128,1024]{1,0:T(8,128)(2,1)S(1)}, u32[]{:S(2)}, u32[]{:S(2)}) collective-permute-start(bf16[128,1024]{1,0:T(8,128)(2,1)S(1)} %collective-permute-done.1.refs_0_), channel_id=1, source_target_pairs={{0,8},{1,25},{2,10},{3,27},{4,12},{5,29},{6,14},{7,31},{8,0},{9,17... | collective-permute-start | bytes 786440 | tf_op jit(solution)/shard_map/ppermute | solution.py:36
  14.1 7.4 %collective-permute-start.4 = (bf16[128,1024]{1,0:T(8,128)(2,1)S(1)}, bf16[128,1024]{1,0:T(8,128)(2,1)S(1)}, u32[]{:S(2)}, u32[]{:S(2)}) collective-permute-start(bf16[128,1024]{1,0:T(8,128)(2,1)S(1)} %collective-permute-done.1.refs_0_), channel_id=1, source_target_pairs={{0,10},{1,31},{2,12},{3,25},{4,14},{5,27},{6,8},{7,29},{8,2},{9,23... | collective-permute-start | bytes 786440 | tf_op jit(solution)/shard_map/ppermute | solution.py:36
  16.7 7.8 %collective-permute-start.7 = (bf16[128,1024]{1,0:T(8,128)(2,1)S(1)}, bf16[128,1024]{1,0:T(8,128)(2,1)S(1)}, u32[]{:S(2)}, u32[]{:S(2)}) collective-permute-start(bf16[128,1024]{1,0:T(8,128)(2,1)S(1)} %collective-permute-done.3.refs_1_), channel_id=1, source_target_pairs={{0,8},{1,25},{2,10},{3,27},{4,12},{5,29},{6,14},{7,31},{8,0},{9,17... | collective-permute-start | bytes 786440 | tf_op jit(solution)/shard_map/ppermute | solution.py:36
  36.4 1.7 %collective-permute-start.8 = (f32[32,128]{1,0:T(8,128)S(1)}, f32[32,128]{1,0:T(8,128)S(1)}, u32[]{:S(2)}, u32[]{:S(2)}) collective-permute-start(f32[32,128]{1,0:T(8,128)S(1)} %get-tuple-element.44.rows), channel_id=1, source_target_pairs={{0,1},{1,0},{2,3},{3,2},{4,5},{5,4},{6,7},{7,6},{8,9},{9,8},{10,11... | collective-permute-start | bytes 49160 | tf_op jit(solution)/shard_map/ppermute | solution.py:36
  38.1 4.1 %collective-permute-start.9 = (f32[24,128]{1,0:T(8,128)S(1)}, f32[24,128]{1,0:T(8,128)S(1)}, u32[]{:S(2)}, u32[]{:S(2)}) collective-permute-start(f32[24,128]{1,0:T(8,128)S(1)} %shard_map.47.rows), channel_id=1, source_target_pairs={{0,16},{1,17},{2,18},{3,19},{4,20},{5,21},{6,22},{7,23},{8,24},{9,... | collective-permute-start | bytes 36872 | tf_op jit(solution)/shard_map/ppermute | solution.py:36

commit v5 on v4

--- a/solution.py
+++ b/solution.py
@@ -240,8 +240,7 @@
         sent[pl.ds(position, 1), :] = best - 0.5 * col_norm[pl.ds(position, 1), :]
 
 
-def last_kernel(received, row_best_held, row_best, col_best):
-    row_best[...] = row_best_held[...]
+def last_kernel(received, col_best):
     col_best[...] = jnp.max(received[...], axis=0, keepdims=True)
 
 
@@ -318,16 +317,14 @@
     received = lax.all_to_all(sent, "wide", 0, 0, axis_index_groups=along_z, tiled=True)
     sent, row_best = call(
         functools.partial(col_best_kernel, scale),
-        (f32(GROUP, LANES), pltpu.VMEM((8, LANES), jnp.float32)),
+        (f32(GROUP, LANES), f32(8, LANES)),
         *scores,
         received,
         col_norm,
         flops=2 * 1024 * 2048,
     )
     received = exchange(sent)
-    row_best, col_best = call(
-        last_kernel, (f32(8, LANES), f32(1, LANES)), received, held(row_best)
-    )
+    col_best = call(last_kernel, f32(1, LANES), received)
     return row_best.reshape(1024), col_best.reshape(LANES)
 
 

time: 69.3 us -> 69.7 us (level)
  no operation moved by 1% of the time
where the time goes in v5:
time: 69.7 us; the launch traced here: 69.5 us
  blocking collectives  34.9 us (50%)
  starting transfers between devices  17.7 us (25%)
  Pallas kernels  12.9 us (19%)
  waiting for transfers between devices  3.21 us (5%)
  between operations  0.72 us (1%)
    all_to_all x2, blocking collectives, exchange(): lax.all_to_all(value, BOTH, 0, 0, axis_index_groups=groups, tiled=True)  19.4 us
    ppermute x10, starting transfers between devices, move(): return lax.ppermute(value, BOTH, pairs)  17.7 us
    all_to_all x1, blocking collectives, body(): lax.all_to_all(sent, 'wide', 0, 0, axis_index_groups=along_z, tiled=True)  15.5 us
    pallas_call x10, Pallas kernels, call(): pl.pallas_call(kernel, out_shape=out_shape, in_specs=[pl.BlockSpec(memory...  12.9 us
    ppermute x10, waiting for transfers between devices, move(): return lax.ppermute(value, BOTH, pairs)  3.21 us
  transfers between devices with their start and end apart: 10, of which 4 were waited for; matrix products, arithmetic and copies ran while one was open for 0% of the time, Pallas kernels for 12%

profile of v5, /device:TPU:1, one launch (start us, length us, event | category | flops | bytes accessed | tf_op | source)
XLA Modules:
  0.0 69.5 jit_solution(14386394931899540069)
XLA Ops:
  0.6 3.3 %collective-permute-start = (bf16[1024,1024]{1,0:T(8,128)(2,1)}, bf16[1024,1024]{1,0:T(8,128)(2,1)S(1)}, u32[]{:S(2)}, u32[]{:S(2)}) collective-permute-start(bf16[1024,1024]{1,0:T(8,128)(2,1)} %sources.1), channel_id=1, source_target_pairs={{0,1},{1,0},{2,3},{3,2},{4,5},{5,4},{6,7},{7,6},{8,9},{9,8},{10,11... | collective-permute-start | bytes 6291464 | tf_op jit(solution)/shard_map/ppermute | solution.py:36
  4.0 0.7 %collective-permute-start.1 = (bf16[128,1024]{1,0:T(8,128)(2,1)}, bf16[128,1024]{1,0:T(8,128)(2,1)S(1)}, u32[]{:S(2)}, u32[]{:S(2)}) collective-permute-start(bf16[128,1024]{1,0:T(8,128)(2,1)} %targets.1), channel_id=1, source_target_pairs={{0,2},{1,7},{2,4},{3,1},{4,6},{5,3},{6,0},{7,5},{8,10},{9,15},{10,... | collective-permute-start | bytes 786440 | tf_op jit(solution)/shard_map/ppermute | solution.py:36
  4.7 2.7 %collective-permute-start.2 = (bf16[128,1024]{1,0:T(8,128)(2,1)}, bf16[128,1024]{1,0:T(8,128)(2,1)S(1)}, u32[]{:S(2)}, u32[]{:S(2)}) collective-permute-start(bf16[128,1024]{1,0:T(8,128)(2,1)} %targets.1), channel_id=1, source_target_pairs={{0,8},{1,25},{2,10},{3,27},{4,12},{5,29},{6,14},{7,31},{8,0},{9,17... | collective-permute-start | bytes 786440 | tf_op jit(solution)/shard_map/ppermute | solution.py:36
  7.4 1.7 %shard_map.41 = (bf16[1024,1024]{1,0:T(8,128)(2,1)S(1)}, bf16[128,1024]{1,0:T(8,128)(2,1)S(1)}) custom-call(bf16[1024,1024]{1,0:T(8,128)(2,1)} %sources.1, bf16[128,1024]{1,0:T(8,128)(2,1)} %targets.1), custom_call_target="tpu_custom_call" | custom-call | bytes 2359296 | tf_op jit(solution)/shard_map/pallas_call | solution.py:87
  9.1 0.1 collective-permute-start.3
  9.2 0.5 collective-permute-done.1.refs_0_
  9.7 2.2 %collective-permute-start.6 = (bf16[128,1024]{1,0:T(8,128)(2,1)S(1)}, bf16[128,1024]{1,0:T(8,128)(2,1)S(1)}, u32[]{:S(2)}, u32[]{:S(2)}) collective-permute-start(bf16[128,1024]{1,0:T(8,128)(2,1)S(1)} %collective-permute-done.1.refs_0_), channel_id=1, source_target_pairs={{0,2},{1,7},{2,4},{3,1},{4,6},{5,3},{6,0},{7,5},{8,10},{9,15},{10,... | collective-permute-start | bytes 786440 | tf_op jit(solution)/shard_map/ppermute | solution.py:36
  11.9 2.2 %collective-permute-start.5 = (bf16[128,1024]{1,0:T(8,128)(2,1)S(1)}, bf16[128,1024]{1,0:T(8,128)(2,1)S(1)}, u32[]{:S(2)}, u32[]{:S(2)}) collective-permute-start(bf16[128,1024]{1,0:T(8,128)(2,1)S(1)} %collective-permute-done.1.refs_0_), channel_id=1, source_target_pairs={{0,8},{1,25},{2,10},{3,27},{4,12},{5,29},{6,14},{7,31},{8,0},{9,17... | collective-permute-start | bytes 786440 | tf_op jit(solution)/shard_map/ppermute | solution.py:36
  14.1 0.0 collective-permute-done.2.refs_1_
  14.1 0.6 collective-permute-start.4
  14.6 0.0 collective-permute-done.s1
  14.6 2.0 %shard_map.42 = (f32[256,2048]{1,0:T(8,128)S(1)}, f32[16,128]{1,0:T(8,128)S(1)}, f32[2,128]{1,0:T(2,128)S(1)}) custom-call(bf16[1024,1024]{1,0:T(8,128)(2,1)S(1)} %get-tuple-element.24.s0, bf16[1024,1024]{1,0:T(8,128)(2,1)S(1)} %collective-permute-done.s1, bf16[128,1024]{1,0:T(8,128)(2,1)S(1)} %get-tuple-element.26.refs_0_, ...), custom_call_target="tpu_custom_call" | custom-call | flops 1073741824 | bytes 4718592 | tf_op jit(solution)/shard_map/pallas_call | solution.py:87
  16.7 0.0 collective-permute-done.3.refs_1_
  16.7 2.1 %collective-permute-start.7 = (bf16[128,1024]{1,0:T(8,128)(2,1)S(1)}, bf16[128,1024]{1,0:T(8,128)(2,1)S(1)}, u32[]{:S(2)}, u32[]{:S(2)}) collective-permute-start(bf16[128,1024]{1,0:T(8,128)(2,1)S(1)} %collective-permute-done.3.refs_1_), channel_id=1, source_target_pairs={{0,8},{1,25},{2,10},{3,27},{4,12},{5,29},{6,14},{7,31},{8,0},{9,17... | collective-permute-start | bytes 786440 | tf_op jit(solution)/shard_map/ppermute | solution.py:36
  18.8 2.0 %shard_map.43 = (f32[256,2048]{1,0:T(8,128)S(1)}, f32[16,128]{1,0:T(8,128)S(1)}, f32[2,128]{1,0:T(2,128)S(1)}) custom-call(bf16[1024,1024]{1,0:T(8,128)(2,1)S(1)} %get-tuple-element.24.s0, bf16[1024,1024]{1,0:T(8,128)(2,1)S(1)} %collective-permute-done.s1, bf16[128,1024]{1,0:T(8,128)(2,1)S(1)} %collective-permute-done.1.refs_0_, ...), custom_call_target="tpu_custom_call" | custom-call | flops 1073741824 | bytes 4718592 | tf_op jit(solution)/shard_map/pallas_call | solution.py:87
  20.8 0.0 collective-permute-done.6.refs_2_
  20.8 0.0 collective-permute-done.5.refs_1_
  20.8 0.7 %collective-permute-done.4.refs_0_ = bf16[128,1024]{1,0:T(8,128)(2,1)S(1)} collective-permute-done((bf16[128,1024]{1,0:T(8,128)(2,1)S(1)}, bf16[128,1024]{1,0:T(8,128)(2,1)S(1)}, u32[]{:S(2)}, u32[]{:S(2)}) %collective-permute-start.4) | collective-permute-done | bytes 262176 | tf_op jit(solution)/shard_map/ppermute | solution.py:36
  21.5 2.9 %shard_map.44 = (f32[384,2048]{1,0:T(8,128)S(1)}, f32[16,128]{1,0:T(8,128)S(1)}, f32[3,128]{1,0:T(4,128)S(1)}) custom-call(bf16[1024,1024]{1,0:T(8,128)(2,1)S(1)} %get-tuple-element.24.s0, bf16[1024,1024]{1,0:T(8,128)(2,1)S(1)} %collective-permute-done.s1, bf16[128,1024]{1,0:T(8,128)(2,1)S(1)} %collective-permute-done.4.refs_0_, ...), custom_call_target="tpu_custom_call" | custom-call | flops 1610612736 | bytes 4980736 | tf_op jit(solution)/shard_map/pallas_call | solution.py:87
  24.4 0.0 collective-permute-done.7.ta
  24.5 1.8 %shard_map.45 = (f32[128,2048]{1,0:T(8,128)S(1)}, f32[16,128]{1,0:T(8,128)S(1)}, f32[64,128]{1,0:T(8,128)S(1)}) custom-call(bf16[1024,1024]{1,0:T(8,128)(2,1)S(1)} %get-tuple-element.24.s0, bf16[1024,1024]{1,0:T(8,128)(2,1)S(1)} %collective-permute-done.s1, bf16[128,1024]{1,0:T(8,128)(2,1)S(1)} %collective-permute-done.7.ta, ...), custom_call_target="tpu_custom_call" | custom-call | flops 536870912 | bytes 4484608 | tf_op jit(solution)/shard_map/pallas_call | solution.py:87
  26.3 9.4 %all_to_all.33 = f32[8,8,128]{2,1,0:T(8,128)S(1)} all-to-all(f32[8,8,128]{2,1,0:T(8,128)S(1)} %bitcast.13), channel_id=1, replica_groups={{0,2,4,6,8,10,12,14},{16,18,20,22,24,26,28,30},{1,3,5,7,25,27,29,31},{1..., dimensions={0} | all-to-all | bytes 65536 | tf_op jit(solution)/shard_map/all_to_all | solution.py:252
  35.6 0.8 %shard_map.46 = (f32[32,128]{1,0:T(8,128)S(1)}, f32[8,128]{1,0:T(8,128)S(1)}) custom-call(f32[256,2048]{1,0:T(8,128)S(1)} %get-tuple-element.27.a0, f32[256,2048]{1,0:T(8,128)S(1)} %get-tuple-element.31.a1, f32[384,2048]{1,0:T(8,128)S(1)} %get-tuple-element.32.a2, f32[128,2048]{1,0:T(8,128)S(1)} %get-tuple-element.39.a3, f32[64,128]{1,0:T(8,128)S(1)} %bitcast.12, ...), custom_call_target="tpu_custom_call" | custom-call | flops 4194304 | bytes 8429568 | tf_op jit(solution)/shard_map/pallas_call | solution.py:87
  36.4 0.8 %collective-permute-start.8 = (f32[32,128]{1,0:T(8,128)S(1)}, f32[32,128]{1,0:T(8,128)S(1)}, u32[]{:S(2)}, u32[]{:S(2)}) collective-permute-start(f32[32,128]{1,0:T(8,128)S(1)} %get-tuple-element.42.rows), channel_id=1, source_target_pairs={{0,1},{1,0},{2,3},{3,2},{4,5},{5,4},{6,7},{7,6},{8,9},{9,8},{10,11... | collective-permute-start | bytes 49160 | tf_op jit(solution)/shard_map/ppermute | solution.py:36
  37.2 0.8 %collective-permute-done.8.core = f32[32,128]{1,0:T(8,128)S(1)} collective-permute-done((f32[32,128]{1,0:T(8,128)S(1)}, f32[32,128]{1,0:T(8,128)S(1)}, u32[]{:S(2)}, u32[]{:S(2)}) %collective-permute-start.8) | collective-permute-done | bytes 16416 | tf_op jit(solution)/shard_map/ppermute | solution.py:36
  38.1 3.0 %collective-permute-start.9 = (f32[24,128]{1,0:T(8,128)S(1)}, f32[24,128]{1,0:T(8,128)S(1)}, u32[]{:S(2)}, u32[]{:S(2)}) collective-permute-start(f32[24,128]{1,0:T(8,128)S(1)} %shard_map.47.rows), channel_id=1, source_target_pairs={{0,16},{1,17},{2,18},{3,19},{4,20},{5,21},{6,22},{7,23},{8,24},{9,... | collective-permute-start | bytes 36872 | tf_op jit(solution)/shard_map/ppermute | solution.py:36
  41.0 1.2 %collective-permute-done.9.far = f32[24,128]{1,0:T(8,128)S(1)} collective-permute-done((f32[24,128]{1,0:T(8,128)S(1)}, f32[24,128]{1,0:T(8,128)S(1)}, u32[]{:S(2)}, u32[]{:S(2)}) %collective-permute-start.9) | collective-permute-done | bytes 12320 | tf_op jit(solution)/shard_map/ppermute | solution.py:36
  42.2 15.5 %all_to_all.34 = f32[8,24,128]{2,1,0:T(8,128)S(1)} all-to-all(f32[8,24,128]{2,1,0:T(8,128)S(1)} %bitcast.11), channel_id=1, replica_groups={{0,32,64,96,128,160,192,224},{16,48,80,112,144,176,208,240},{1,33,65,97..., dimensions={0} | all-to-all | bytes 196608 | tf_op jit(solution)/shard_map/all_to_all | solution.py:317
  57.7 1.2 %shard_map.49 = (f32[8,128]{1,0:T(8,128)S(1)}, f32[8,128]{1,0:T(8,128)}) custom-call(f32[256,2048]{1,0:T(8,128)S(1)} %get-tuple-element.27.a0, f32[256,2048]{1,0:T(8,128)S(1)} %get-tuple-element.31.a1, f32[384,2048]{1,0:T(8,128)S(1)} %get-tuple-element.32.a2, f32[128,2048]{1,0:T(8,128)S(1)} %get-tuple-element.39.a3, f32[192,128]{1,0:T(8,128)S(1)} %bitcast.10, ...), custom_call_target="tpu_custom_call" | custom-call | flops 4194304 | bytes 8491008 | tf_op jit(solution)/shard_map/pallas_call | solution.py:87
  58.9 10.1 %all_to_all.35 = f32[8,1,128]{2,1,0:T(1,128)S(1)} all-to-all(f32[8,1,128]{2,1,0:T(1,128)S(1)} %bitcast.15), channel_id=1, replica_groups={{0,2,4,6,8,10,12,14},{16,18,20,22,24,26,28,30},{1,3,5,7,25,27,29,31},{1..., dimensions={0} | all-to-all | bytes 8192 | tf_op jit(solution)/shard_map/all_to_all | solution.py:252
  69.0 0.5 shard_map.50
  (2 shorter events, 0.0 us)
Async XLA Ops:
  0.6 14.0 %collective-permute-start = (bf16[1024,1024]{1,0:T(8,128)(2,1)}, bf16[1024,1024]{1,0:T(8,128)(2,1)S(1)}, u32[]{:S(2)}, u32[]{:S(2)}) collective-permute-start(bf16[1024,1024]{1,0:T(8,128)(2,1)} %sources.1), channel_id=1, source_target_pairs={{0,1},{1,0},{2,3},{3,2},{4,5},{5,4},{6,7},{7,6},{8,9},{9,8},{10,11... | collective-permute-start | bytes 6291464 | tf_op jit(solution)/shard_map/ppermute | solution.py:36
  4.0 5.7 %collective-permute-start.1 = (bf16[128,1024]{1,0:T(8,128)(2,1)}, bf16[128,1024]{1,0:T(8,128)(2,1)S(1)}, u32[]{:S(2)}, u32[]{:S(2)}) collective-permute-start(bf16[128,1024]{1,0:T(8,128)(2,1)} %targets.1), channel_id=1, source_target_pairs={{0,2},{1,7},{2,4},{3,1},{4,6},{5,3},{6,0},{7,5},{8,10},{9,15},{10,... | collective-permute-start | bytes 786440 | tf_op jit(solution)/shard_map/ppermute | solution.py:36
  4.7 9.4 %collective-permute-start.2 = (bf16[128,1024]{1,0:T(8,128)(2,1)}, bf16[128,1024]{1,0:T(8,128)(2,1)S(1)}, u32[]{:S(2)}, u32[]{:S(2)}) collective-permute-start(bf16[128,1024]{1,0:T(8,128)(2,1)} %targets.1), channel_id=1, source_target_pairs={{0,8},{1,25},{2,10},{3,27},{4,12},{5,29},{6,14},{7,31},{8,0},{9,17... | collective-permute-start | bytes 786440 | tf_op jit(solution)/shard_map/ppermute | solution.py:36
  9.1 7.6 %collective-permute-start.3 = (bf16[128,1024]{1,0:T(8,128)(2,1)S(1)}, bf16[128,1024]{1,0:T(8,128)(2,1)S(1)}, u32[]{:S(2)}, u32[]{:S(2)}) collective-permute-start(bf16[128,1024]{1,0:T(8,128)(2,1)S(1)} %get-tuple-element.26.refs_0_), channel_id=1, source_target_pairs={{0,6},{1,3},{2,0},{3,5},{4,2},{5,7},{6,4},{7,1},{8,14},{9,11},{10,... | collective-permute-start | bytes 786440 | tf_op jit(solution)/shard_map/ppermute | solution.py:36
  9.7 11.1 %collective-permute-start.6 = (bf16[128,1024]{1,0:T(8,128)(2,1)S(1)}, bf16[128,1024]{1,0:T(8,128)(2,1)S(1)}, u32[]{:S(2)}, u32[]{:S(2)}) collective-permute-start(bf16[128,1024]{1,0:T(8,128)(2,1)S(1)} %collective-permute-done.1.refs_0_), channel_id=1, source_target_pairs={{0,2},{1,7},{2,4},{3,1},{4,6},{5,3},{6,0},{7,5},{8,10},{9,15},{10,... | collective-permute-start | bytes 786440 | tf_op jit(solution)/shard_map/ppermute | solution.py:36
  11.9 8.9 %collective-permute-start.5 = (bf16[128,1024]{1,0:T(8,128)(2,1)S(1)}, bf16[128,1024]{1,0:T(8,128)(2,1)S(1)}, u32[]{:S(2)}, u32[]{:S(2)}) collective-permute-start(bf16[128,1024]{1,0:T(8,128)(2,1)S(1)} %collective-permute-done.1.refs_0_), channel_id=1, source_target_pairs={{0,8},{1,25},{2,10},{3,27},{4,12},{5,29},{6,14},{7,31},{8,0},{9,17... | collective-permute-start | bytes 786440 | tf_op jit(solution)/shard_map/ppermute | solution.py:36
  14.1 7.4 %collective-permute-start.4 = (bf16[128,1024]{1,0:T(8,128)(2,1)S(1)}, bf16[128,1024]{1,0:T(8,128)(2,1)S(1)}, u32[]{:S(2)}, u32[]{:S(2)}) collective-permute-start(bf16[128,1024]{1,0:T(8,128)(2,1)S(1)} %collective-permute-done.1.refs_0_), channel_id=1, source_target_pairs={{0,10},{1,31},{2,12},{3,25},{4,14},{5,27},{6,8},{7,29},{8,2},{9,23... | collective-permute-start | bytes 786440 | tf_op jit(solution)/shard_map/ppermute | solution.py:36
  16.7 7.8 %collective-permute-start.7 = (bf16[128,1024]{1,0:T(8,128)(2,1)S(1)}, bf16[128,1024]{1,0:T(8,128)(2,1)S(1)}, u32[]{:S(2)}, u32[]{:S(2)}) collective-permute-start(bf16[128,1024]{1,0:T(8,128)(2,1)S(1)} %collective-permute-done.3.refs_1_), channel_id=1, source_target_pairs={{0,8},{1,25},{2,10},{3,27},{4,12},{5,29},{6,14},{7,31},{8,0},{9,17... | collective-permute-start | bytes 786440 | tf_op jit(solution)/shard_map/ppermute | solution.py:36
  36.4 1.7 %collective-permute-start.8 = (f32[32,128]{1,0:T(8,128)S(1)}, f32[32,128]{1,0:T(8,128)S(1)}, u32[]{:S(2)}, u32[]{:S(2)}) collective-permute-start(f32[32,128]{1,0:T(8,128)S(1)} %get-tuple-element.42.rows), channel_id=1, source_target_pairs={{0,1},{1,0},{2,3},{3,2},{4,5},{5,4},{6,7},{7,6},{8,9},{9,8},{10,11... | collective-permute-start | bytes 49160 | tf_op jit(solution)/shard_map/ppermute | solution.py:36
  38.1 4.1 %collective-permute-start.9 = (f32[24,128]{1,0:T(8,128)S(1)}, f32[24,128]{1,0:T(8,128)S(1)}, u32[]{:S(2)}, u32[]{:S(2)}) collective-permute-start(f32[24,128]{1,0:T(8,128)S(1)} %shard_map.47.rows), channel_id=1, source_target_pairs={{0,16},{1,17},{2,18},{3,19},{4,20},{5,21},{6,22},{7,23},{8,24},{9,... | collective-permute-start | bytes 36872 | tf_op jit(solution)/shard_map/ppermute | solution.py:36

commit v6 on v5

--- a/solution.py
+++ b/solution.py
@@ -238,10 +238,6 @@
         best = as_row(jnp.max(best, axis=1, keepdims=True)) * scale
         position = owner(place, slot)
         sent[pl.ds(position, 1), :] = best - 0.5 * col_norm[pl.ds(position, 1), :]
-
-
-def last_kernel(received, col_best):
-    col_best[...] = jnp.max(received[...], axis=0, keepdims=True)
 
 
 def body(sources, targets):
@@ -324,7 +320,7 @@
         flops=2 * 1024 * 2048,
     )
     received = exchange(sent)
-    col_best = call(last_kernel, f32(1, LANES), received)
+    col_best = jnp.max(received, axis=0)
     return row_best.reshape(1024), col_best.reshape(LANES)
 
 

time: 69.7 us -> 69.8 us (level)
    pallas_call x10 -> x9, Pallas kernels: 12.9 us -> 12.4 us  [call(): pl.pallas_call(kernel, out_shape=out_shape, in_specs=[pl.BlockSpec(memory...]
where the time goes in v6:
time: 69.8 us; the launch traced here: 69.5 us
  blocking collectives  34.9 us (50%)
  starting transfers between devices  17.7 us (25%)
  Pallas kernels  12.4 us (18%)
  waiting for transfers between devices  3.21 us (5%)
  between operations  0.72 us (1%)
    all_to_all x2, blocking collectives, exchange(): lax.all_to_all(value, BOTH, 0, 0, axis_index_groups=groups, tiled=True)  19.4 us
    ppermute x10, starting transfers between devices, move(): return lax.ppermute(value, BOTH, pairs)  17.7 us
    all_to_all x1, blocking collectives, body(): lax.all_to_all(sent, 'wide', 0, 0, axis_index_groups=along_z, tiled=True)  15.5 us
    pallas_call x9, Pallas kernels, call(): pl.pallas_call(kernel, out_shape=out_shape, in_specs=[pl.BlockSpec(memory...  12.4 us
    ppermute x10, waiting for transfers between devices, move(): return lax.ppermute(value, BOTH, pairs)  3.21 us
  transfers between devices with their start and end apart: 10, of which 4 were waited for; matrix products, arithmetic and copies ran while one was open for 0% of the time, Pallas kernels for 12%

profile of v6, /device:TPU:1, one launch (start us, length us, event | category | flops | bytes accessed | tf_op | source)
XLA Modules:
  0.0 69.5 jit_solution(17593129336230530141)
XLA Ops:
  0.6 3.3 %collective-permute-start = (bf16[1024,1024]{1,0:T(8,128)(2,1)}, bf16[1024,1024]{1,0:T(8,128)(2,1)S(1)}, u32[]{:S(2)}, u32[]{:S(2)}) collective-permute-start(bf16[1024,1024]{1,0:T(8,128)(2,1)} %sources.1), channel_id=1, source_target_pairs={{0,1},{1,0},{2,3},{3,2},{4,5},{5,4},{6,7},{7,6},{8,9},{9,8},{10,11... | collective-permute-start | bytes 6291464 | tf_op jit(solution)/shard_map/ppermute | solution.py:36
  4.0 0.7 %collective-permute-start.1 = (bf16[128,1024]{1,0:T(8,128)(2,1)}, bf16[128,1024]{1,0:T(8,128)(2,1)S(1)}, u32[]{:S(2)}, u32[]{:S(2)}) collective-permute-start(bf16[128,1024]{1,0:T(8,128)(2,1)} %targets.1), channel_id=1, source_target_pairs={{0,2},{1,7},{2,4},{3,1},{4,6},{5,3},{6,0},{7,5},{8,10},{9,15},{10,... | collective-permute-start | bytes 786440 | tf_op jit(solution)/shard_map/ppermute | solution.py:36
  4.7 2.7 %collective-permute-start.2 = (bf16[128,1024]{1,0:T(8,128)(2,1)}, bf16[128,1024]{1,0:T(8,128)(2,1)S(1)}, u32[]{:S(2)}, u32[]{:S(2)}) collective-permute-start(bf16[128,1024]{1,0:T(8,128)(2,1)} %targets.1), channel_id=1, source_target_pairs={{0,8},{1,25},{2,10},{3,27},{4,12},{5,29},{6,14},{7,31},{8,0},{9,17... | collective-permute-start | bytes 786440 | tf_op jit(solution)/shard_map/ppermute | solution.py:36
  7.4 1.7 %shard_map.41 = (bf16[1024,1024]{1,0:T(8,128)(2,1)S(1)}, bf16[128,1024]{1,0:T(8,128)(2,1)S(1)}) custom-call(bf16[1024,1024]{1,0:T(8,128)(2,1)} %sources.1, bf16[128,1024]{1,0:T(8,128)(2,1)} %targets.1), custom_call_target="tpu_custom_call" | custom-call | bytes 2359296 | tf_op jit(solution)/shard_map/pallas_call | solution.py:87
  9.1 0.1 collective-permute-start.3
  9.2 0.5 collective-permute-done.1.refs_0_
  9.7 2.2 %collective-permute-start.6 = (bf16[128,1024]{1,0:T(8,128)(2,1)S(1)}, bf16[128,1024]{1,0:T(8,128)(2,1)S(1)}, u32[]{:S(2)}, u32[]{:S(2)}) collective-permute-start(bf16[128,1024]{1,0:T(8,128)(2,1)S(1)} %collective-permute-done.1.refs_0_), channel_id=1, source_target_pairs={{0,2},{1,7},{2,4},{3,1},{4,6},{5,3},{6,0},{7,5},{8,10},{9,15},{10,... | collective-permute-start | bytes 786440 | tf_op jit(solution)/shard_map/ppermute | solution.py:36
  11.9 2.2 %collective-permute-start.5 = (bf16[128,1024]{1,0:T(8,128)(2,1)S(1)}, bf16[128,1024]{1,0:T(8,128)(2,1)S(1)}, u32[]{:S(2)}, u32[]{:S(2)}) collective-permute-start(bf16[128,1024]{1,0:T(8,128)(2,1)S(1)} %collective-permute-done.1.refs_0_), channel_id=1, source_target_pairs={{0,8},{1,25},{2,10},{3,27},{4,12},{5,29},{6,14},{7,31},{8,0},{9,17... | collective-permute-start | bytes 786440 | tf_op jit(solution)/shard_map/ppermute | solution.py:36
  14.1 0.0 collective-permute-done.2.refs_1_
  14.1 0.6 collective-permute-start.4
  14.6 0.0 collective-permute-done.s1
  14.6 2.0 %shard_map.42 = (f32[256,2048]{1,0:T(8,128)S(1)}, f32[16,128]{1,0:T(8,128)S(1)}, f32[2,128]{1,0:T(2,128)S(1)}) custom-call(bf16[1024,1024]{1,0:T(8,128)(2,1)S(1)} %get-tuple-element.24.s0, bf16[1024,1024]{1,0:T(8,128)(2,1)S(1)} %collective-permute-done.s1, bf16[128,1024]{1,0:T(8,128)(2,1)S(1)} %get-tuple-element.26.refs_0_, ...), custom_call_target="tpu_custom_call" | custom-call | flops 1073741824 | bytes 4718592 | tf_op jit(solution)/shard_map/pallas_call | solution.py:87
  16.7 0.0 collective-permute-done.3.refs_1_
  16.7 2.1 %collective-permute-start.7 = (bf16[128,1024]{1,0:T(8,128)(2,1)S(1)}, bf16[128,1024]{1,0:T(8,128)(2,1)S(1)}, u32[]{:S(2)}, u32[]{:S(2)}) collective-permute-start(bf16[128,1024]{1,0:T(8,128)(2,1)S(1)} %collective-permute-done.3.refs_1_), channel_id=1, source_target_pairs={{0,8},{1,25},{2,10},{3,27},{4,12},{5,29},{6,14},{7,31},{8,0},{9,17... | collective-permute-start | bytes 786440 | tf_op jit(solution)/shard_map/ppermute | solution.py:36
  18.8 2.0 %shard_map.43 = (f32[256,2048]{1,0:T(8,128)S(1)}, f32[16,128]{1,0:T(8,128)S(1)}, f32[2,128]{1,0:T(2,128)S(1)}) custom-call(bf16[1024,1024]{1,0:T(8,128)(2,1)S(1)} %get-tuple-element.24.s0, bf16[1024,1024]{1,0:T(8,128)(2,1)S(1)} %collective-permute-done.s1, bf16[128,1024]{1,0:T(8,128)(2,1)S(1)} %collective-permute-done.1.refs_0_, ...), custom_call_target="tpu_custom_call" | custom-call | flops 1073741824 | bytes 4718592 | tf_op jit(solution)/shard_map/pallas_call | solution.py:87
  20.8 0.0 collective-permute-done.6.refs_2_
  20.8 0.0 collective-permute-done.5.refs_1_
  20.8 0.7 %collective-permute-done.4.refs_0_ = bf16[128,1024]{1,0:T(8,128)(2,1)S(1)} collective-permute-done((bf16[128,1024]{1,0:T(8,128)(2,1)S(1)}, bf16[128,1024]{1,0:T(8,128)(2,1)S(1)}, u32[]{:S(2)}, u32[]{:S(2)}) %collective-permute-start.4) | collective-permute-done | bytes 262176 | tf_op jit(solution)/shard_map/ppermute | solution.py:36
  21.5 2.9 %shard_map.44 = (f32[384,2048]{1,0:T(8,128)S(1)}, f32[16,128]{1,0:T(8,128)S(1)}, f32[3,128]{1,0:T(4,128)S(1)}) custom-call(bf16[1024,1024]{1,0:T(8,128)(2,1)S(1)} %get-tuple-element.24.s0, bf16[1024,1024]{1,0:T(8,128)(2,1)S(1)} %collective-permute-done.s1, bf16[128,1024]{1,0:T(8,128)(2,1)S(1)} %collective-permute-done.4.refs_0_, ...), custom_call_target="tpu_custom_call" | custom-call | flops 1610612736 | bytes 4980736 | tf_op jit(solution)/shard_map/pallas_call | solution.py:87
  24.4 0.0 collective-permute-done.7.ta
  24.5 1.8 %shard_map.45 = (f32[128,2048]{1,0:T(8,128)S(1)}, f32[16,128]{1,0:T(8,128)S(1)}, f32[64,128]{1,0:T(8,128)S(1)}) custom-call(bf16[1024,1024]{1,0:T(8,128)(2,1)S(1)} %get-tuple-element.24.s0, bf16[1024,1024]{1,0:T(8,128)(2,1)S(1)} %collective-permute-done.s1, bf16[128,1024]{1,0:T(8,128)(2,1)S(1)} %collective-permute-done.7.ta, ...), custom_call_target="tpu_custom_call" | custom-call | flops 536870912 | bytes 4484608 | tf_op jit(solution)/shard_map/pallas_call | solution.py:87
  26.3 9.4 %all_to_all.31 = f32[8,8,128]{2,1,0:T(8,128)S(1)} all-to-all(f32[8,8,128]{2,1,0:T(8,128)S(1)} %bitcast.11), channel_id=1, replica_groups={{0,2,4,6,8,10,12,14},{16,18,20,22,24,26,28,30},{1,3,5,7,25,27,29,31},{1..., dimensions={0} | all-to-all | bytes 65536 | tf_op jit(solution)/shard_map/all_to_all | solution.py:248
  35.6 0.8 %shard_map.46 = (f32[32,128]{1,0:T(8,128)S(1)}, f32[8,128]{1,0:T(8,128)S(1)}) custom-call(f32[256,2048]{1,0:T(8,128)S(1)} %get-tuple-element.27.a0, f32[256,2048]{1,0:T(8,128)S(1)} %get-tuple-element.31.a1, f32[384,2048]{1,0:T(8,128)S(1)} %get-tuple-element.32.a2, f32[128,2048]{1,0:T(8,128)S(1)} %get-tuple-element.39.a3, f32[64,128]{1,0:T(8,128)S(1)} %bitcast.10, ...), custom_call_target="tpu_custom_call" | custom-call | flops 4194304 | bytes 8429568 | tf_op jit(solution)/shard_map/pallas_call | solution.py:87
  36.4 0.8 %collective-permute-start.8 = (f32[32,128]{1,0:T(8,128)S(1)}, f32[32,128]{1,0:T(8,128)S(1)}, u32[]{:S(2)}, u32[]{:S(2)}) collective-permute-start(f32[32,128]{1,0:T(8,128)S(1)} %get-tuple-element.42.rows), channel_id=1, source_target_pairs={{0,1},{1,0},{2,3},{3,2},{4,5},{5,4},{6,7},{7,6},{8,9},{9,8},{10,11... | collective-permute-start | bytes 49160 | tf_op jit(solution)/shard_map/ppermute | solution.py:36
  37.2 0.8 %collective-permute-done.8.core = f32[32,128]{1,0:T(8,128)S(1)} collective-permute-done((f32[32,128]{1,0:T(8,128)S(1)}, f32[32,128]{1,0:T(8,128)S(1)}, u32[]{:S(2)}, u32[]{:S(2)}) %collective-permute-start.8) | collective-permute-done | bytes 16416 | tf_op jit(solution)/shard_map/ppermute | solution.py:36
  38.1 3.0 %collective-permute-start.9 = (f32[24,128]{1,0:T(8,128)S(1)}, f32[24,128]{1,0:T(8,128)S(1)}, u32[]{:S(2)}, u32[]{:S(2)}) collective-permute-start(f32[24,128]{1,0:T(8,128)S(1)} %shard_map.47.rows), channel_id=1, source_target_pairs={{0,16},{1,17},{2,18},{3,19},{4,20},{5,21},{6,22},{7,23},{8,24},{9,... | collective-permute-start | bytes 36872 | tf_op jit(solution)/shard_map/ppermute | solution.py:36
  41.0 1.2 %collective-permute-done.9.far = f32[24,128]{1,0:T(8,128)S(1)} collective-permute-done((f32[24,128]{1,0:T(8,128)S(1)}, f32[24,128]{1,0:T(8,128)S(1)}, u32[]{:S(2)}, u32[]{:S(2)}) %collective-permute-start.9) | collective-permute-done | bytes 12320 | tf_op jit(solution)/shard_map/ppermute | solution.py:36
  42.2 15.5 %all_to_all.32 = f32[8,24,128]{2,1,0:T(8,128)S(1)} all-to-all(f32[8,24,128]{2,1,0:T(8,128)S(1)} %bitcast.9), channel_id=1, replica_groups={{0,32,64,96,128,160,192,224},{16,48,80,112,144,176,208,240},{1,33,65,97..., dimensions={0} | all-to-all | bytes 196608 | tf_op jit(solution)/shard_map/all_to_all | solution.py:313
  57.7 1.2 %shard_map.49 = (f32[8,128]{1,0:T(8,128)S(1)}, f32[8,128]{1,0:T(8,128)}) custom-call(f32[256,2048]{1,0:T(8,128)S(1)} %get-tuple-element.27.a0, f32[256,2048]{1,0:T(8,128)S(1)} %get-tuple-element.31.a1, f32[384,2048]{1,0:T(8,128)S(1)} %get-tuple-element.32.a2, f32[128,2048]{1,0:T(8,128)S(1)} %get-tuple-element.39.a3, f32[192,128]{1,0:T(8,128)S(1)} %bitcast.8, ...), custom_call_target="tpu_custom_call" | custom-call | flops 4194304 | bytes 8491008 | tf_op jit(solution)/shard_map/pallas_call | solution.py:87
  58.9 10.1 %all_to_all.33 = f32[8,1,128]{2,1,0:T(1,128)S(1)} all-to-all(f32[8,1,128]{2,1,0:T(1,128)S(1)} %bitcast.12), channel_id=1, replica_groups={{0,2,4,6,8,10,12,14},{16,18,20,22,24,26,28,30},{1,3,5,7,25,27,29,31},{1..., dimensions={0} | all-to-all | bytes 8192 | tf_op jit(solution)/shard_map/all_to_all | solution.py:248
  69.0 0.5 reduce_max.9
  (2 shorter events, 0.0 us)
Async XLA Ops:
  0.6 14.0 %collective-permute-start = (bf16[1024,1024]{1,0:T(8,128)(2,1)}, bf16[1024,1024]{1,0:T(8,128)(2,1)S(1)}, u32[]{:S(2)}, u32[]{:S(2)}) collective-permute-start(bf16[1024,1024]{1,0:T(8,128)(2,1)} %sources.1), channel_id=1, source_target_pairs={{0,1},{1,0},{2,3},{3,2},{4,5},{5,4},{6,7},{7,6},{8,9},{9,8},{10,11... | collective-permute-start | bytes 6291464 | tf_op jit(solution)/shard_map/ppermute | solution.py:36
  4.0 5.7 %collective-permute-start.1 = (bf16[128,1024]{1,0:T(8,128)(2,1)}, bf16[128,1024]{1,0:T(8,128)(2,1)S(1)}, u32[]{:S(2)}, u32[]{:S(2)}) collective-permute-start(bf16[128,1024]{1,0:T(8,128)(2,1)} %targets.1), channel_id=1, source_target_pairs={{0,2},{1,7},{2,4},{3,1},{4,6},{5,3},{6,0},{7,5},{8,10},{9,15},{10,... | collective-permute-start | bytes 786440 | tf_op jit(solution)/shard_map/ppermute | solution.py:36
  4.7 9.4 %collective-permute-start.2 = (bf16[128,1024]{1,0:T(8,128)(2,1)}, bf16[128,1024]{1,0:T(8,128)(2,1)S(1)}, u32[]{:S(2)}, u32[]{:S(2)}) collective-permute-start(bf16[128,1024]{1,0:T(8,128)(2,1)} %targets.1), channel_id=1, source_target_pairs={{0,8},{1,25},{2,10},{3,27},{4,12},{5,29},{6,14},{7,31},{8,0},{9,17... | collective-permute-start | bytes 786440 | tf_op jit(solution)/shard_map/ppermute | solution.py:36
  9.1 7.6 %collective-permute-start.3 = (bf16[128,1024]{1,0:T(8,128)(2,1)S(1)}, bf16[128,1024]{1,0:T(8,128)(2,1)S(1)}, u32[]{:S(2)}, u32[]{:S(2)}) collective-permute-start(bf16[128,1024]{1,0:T(8,128)(2,1)S(1)} %get-tuple-element.26.refs_0_), channel_id=1, source_target_pairs={{0,6},{1,3},{2,0},{3,5},{4,2},{5,7},{6,4},{7,1},{8,14},{9,11},{10,... | collective-permute-start | bytes 786440 | tf_op jit(solution)/shard_map/ppermute | solution.py:36
  9.7 11.1 %collective-permute-start.6 = (bf16[128,1024]{1,0:T(8,128)(2,1)S(1)}, bf16[128,1024]{1,0:T(8,128)(2,1)S(1)}, u32[]{:S(2)}, u32[]{:S(2)}) collective-permute-start(bf16[128,1024]{1,0:T(8,128)(2,1)S(1)} %collective-permute-done.1.refs_0_), channel_id=1, source_target_pairs={{0,2},{1,7},{2,4},{3,1},{4,6},{5,3},{6,0},{7,5},{8,10},{9,15},{10,... | collective-permute-start | bytes 786440 | tf_op jit(solution)/shard_map/ppermute | solution.py:36
  11.9 8.9 %collective-permute-start.5 = (bf16[128,1024]{1,0:T(8,128)(2,1)S(1)}, bf16[128,1024]{1,0:T(8,128)(2,1)S(1)}, u32[]{:S(2)}, u32[]{:S(2)}) collective-permute-start(bf16[128,1024]{1,0:T(8,128)(2,1)S(1)} %collective-permute-done.1.refs_0_), channel_id=1, source_target_pairs={{0,8},{1,25},{2,10},{3,27},{4,12},{5,29},{6,14},{7,31},{8,0},{9,17... | collective-permute-start | bytes 786440 | tf_op jit(solution)/shard_map/ppermute | solution.py:36
  14.1 7.4 %collective-permute-start.4 = (bf16[128,1024]{1,0:T(8,128)(2,1)S(1)}, bf16[128,1024]{1,0:T(8,128)(2,1)S(1)}, u32[]{:S(2)}, u32[]{:S(2)}) collective-permute-start(bf16[128,1024]{1,0:T(8,128)(2,1)S(1)} %collective-permute-done.1.refs_0_), channel_id=1, source_target_pairs={{0,10},{1,31},{2,12},{3,25},{4,14},{5,27},{6,8},{7,29},{8,2},{9,23... | collective-permute-start | bytes 786440 | tf_op jit(solution)/shard_map/ppermute | solution.py:36
  16.7 7.8 %collective-permute-start.7 = (bf16[128,1024]{1,0:T(8,128)(2,1)S(1)}, bf16[128,1024]{1,0:T(8,128)(2,1)S(1)}, u32[]{:S(2)}, u32[]{:S(2)}) collective-permute-start(bf16[128,1024]{1,0:T(8,128)(2,1)S(1)} %collective-permute-done.3.refs_1_), channel_id=1, source_target_pairs={{0,8},{1,25},{2,10},{3,27},{4,12},{5,29},{6,14},{7,31},{8,0},{9,17... | collective-permute-start | bytes 786440 | tf_op jit(solution)/shard_map/ppermute | solution.py:36
  36.4 1.7 %collective-permute-start.8 = (f32[32,128]{1,0:T(8,128)S(1)}, f32[32,128]{1,0:T(8,128)S(1)}, u32[]{:S(2)}, u32[]{:S(2)}) collective-permute-start(f32[32,128]{1,0:T(8,128)S(1)} %get-tuple-element.42.rows), channel_id=1, source_target_pairs={{0,1},{1,0},{2,3},{3,2},{4,5},{5,4},{6,7},{7,6},{8,9},{9,8},{10,11... | collective-permute-start | bytes 49160 | tf_op jit(solution)/shard_map/ppermute | solution.py:36
  38.1 4.1 %collective-permute-start.9 = (f32[24,128]{1,0:T(8,128)S(1)}, f32[24,128]{1,0:T(8,128)S(1)}, u32[]{:S(2)}, u32[]{:S(2)}) collective-permute-start(f32[24,128]{1,0:T(8,128)S(1)} %shard_map.47.rows), channel_id=1, source_target_pairs={{0,16},{1,17},{2,18},{3,19},{4,20},{5,21},{6,22},{7,23},{8,24},{9,... | collective-permute-start | bytes 36872 | tf_op jit(solution)/shard_map/ppermute | solution.py:36
